TPU v7x, 256 devices: a whole 4x4x8 slice. The times are simulated.
256 devices in a mesh: inst: 16 (over z, core), tp: 16 (over x, y).
Axes of the slice: x: 4, y: 4, z: 8, core: 2. Of those that a mesh axis runs over, the one named last changes fastest.
Arguments:
- hidden_in: bfloat16 [2, 2048, 8192], P(None, 'inst', 'tp'), may hold values from -128 to 128
- norm_gain: bfloat16 [8192], P('tp'), may hold values from 0.5 to 1.5
- query_weight: bfloat16 [8192, 4096], P(None, 'tp'), may hold values from -0.0625 to 0.0625
- w_key: bfloat16 [8192, 512], P(None, 'tp'), may hold values from -0.0625 to 0.0625
- value_weight: bfloat16 [8192, 512], P(None, 'tp'), may hold values from -0.0625 to 0.0625
- w_output: bfloat16 [4096, 8192], P('tp'), may hold values from -0.25 to 0.25
- paired_down_matrices: bfloat16 [128, 8192, 128], P('inst', 'tp'), may hold values from -0.0625 to 0.0625
- query_up_matrices: bfloat16 [128, 64, 4096], P('inst', None, 'tp'), may hold values from -0.75 to 0.75
- value_up_matrices: bfloat16 [128, 64, 512], P('inst', None, 'tp'), may hold values from -0.75 to 0.75
- output_down_matrices: bfloat16 [128, 64, 4096], P('inst', None, 'tp'), may hold values from -0.25 to 0.25
- output_up_matrices: bfloat16 [128, 64, 8192], P('inst', None, 'tp'), may hold values from -0.75 to 0.75
- key_cache: bfloat16 [2048, 64, 512], P(('inst', 'tp')), may hold values from -160 to 160
- value_cache: bfloat16 [2048, 64, 512], P(('inst', 'tp')), may hold values from -6 to 6
- cache_lengths: int32 [2048], P(('inst', 'tp')), may hold values from 1 to 64, as said below
- row_adapter: int32 [2048], P('inst'), may hold values from 0 to 127, as said below
- old_slot: int32 [128], replicated, may hold values from 0 to 127, as said below
- new_slot: int32 [128], replicated, may hold values from 0 to 127, as said below
Outputs:
- block_out: bfloat16 [2, 2048, 8192], P(None, 'inst', 'tp')
Inputs may be any that keep to these rules, and one draw needn't show every extreme that they name: Each value appears once: adapter a is stored in slot old_slot[a] of the adapter arrays, and slot k belongs to instance k // 8. Each value appears once: after migration adapter a sits in slot new_slot[a], on instance new_slot[a] // 8. No instance sends more than one adapter to any one instance, itself included. `row_adapter`: the rows of instance i (rows i * 128 to (i + 1) * 128 - 1) name only adapters that new_slot places on instance i, each of them at least once; the rows of one adapter are contiguous, in increasing order of its new slot. `cache_lengths`: among the rows of each instance at least one has exactly 64.
All inputs are finite; a program needn't handle non-finite values.
Results may differ from a plain program's by a relative error of at most 0.019.
The roundings to bfloat16 on the way count: a program that leaves them out, or rounds other values in their place, can miss the bound.
Values may be sent and summed in bfloat16 or wider, within the bound.
A program may use at most 128 MiB of HBM per device.

v0:
```python
import math

import jax
import jax.numpy as jnp
from jax import lax
from jax.sharding import PartitionSpec as P

HEADS = 32
KV_HEADS = 4
HD = 128
ADAPTER_RANK = 64


ADAPTER_SCALING = 0.5
NORM_EPS = 1e-05
ROPE_BASE = 500000.0


def rotary(vectors, positions):
    half_width = vectors.shape[-1] // 2
    frequency = ROPE_BASE ** (-jnp.arange(half_width, dtype=jnp.float32) / half_width)
    angles = positions[:, None, None] * frequency[None, None, :]
    cosine = jnp.cos(angles)
    sine_part = jnp.sin(angles)
    first_half = vectors[..., :half_width]
    second_half = vectors[..., half_width:]
    return jnp.concatenate(
        [
            first_half * cosine - second_half * sine_part,
            second_half * cosine + first_half * sine_part,
        ],
        axis=-1,
    )


def lookup(values_table, wanted):
    matches = wanted[:, None] == jnp.arange(values_table.shape[0], dtype=jnp.int32)[None, :]
    return jnp.sum(jnp.where(matches, values_table[None, :], 0), axis=1)


def owner_of(slot_table, wanted):
    matches = slot_table[None, :] == wanted[:, None]
    adapter_ids = jnp.arange(slot_table.shape[0], dtype=jnp.int32)
    return jnp.sum(jnp.where(matches, adapter_ids[None, :], 0), axis=1)


def select_slots(per_slot, chosen):
    return jnp.sum(jnp.where(jnp.transpose(chosen)[:, :, None], per_slot, 0.0), axis=0)


def route_slots(stored, routing):
    return jnp.einsum("jc,cab->jab", routing, stored, preferred_element_type=jnp.float32).astype(
        jnp.bfloat16
    )


def attend_rows(query_vectors, keys_new, values_new, key_rows, value_rows, lengths):
    row_count = query_vectors.shape[0]
    group_size = HEADS // KV_HEADS
    positions_held = key_rows.shape[1]
    score_scale = 1.0 / math.sqrt(HD)
    grouped = query_vectors.reshape(row_count, KV_HEADS, group_size, HD)
    cached_keys = key_rows.reshape(row_count, positions_held, KV_HEADS, HD)
    cached_values = value_rows.reshape(row_count, positions_held, KV_HEADS, HD)
    cache_scores = (
        jnp.einsum("rgqd,rlgd->rgql", grouped, cached_keys, preferred_element_type=jnp.float32)
        * score_scale
    )
    live_keys = jnp.arange(positions_held, dtype=jnp.int32)[None, :] < lengths[:, None]
    cache_scores = jnp.where(live_keys[:, None, None, :], cache_scores, -jnp.inf)
    fresh_scores = (
        jnp.einsum("rgqd,rngd->rgqn", grouped, keys_new, preferred_element_type=jnp.float32)
        * score_scale
    )
    row_top = jnp.maximum(
        jnp.max(cache_scores, axis=3, keepdims=True), jnp.max(fresh_scores, axis=3, keepdims=True)
    )
    cache_powers = jnp.exp(cache_scores - row_top)
    fresh_powers = jnp.exp(fresh_scores - row_top)
    denominator = jnp.sum(cache_powers, axis=3, keepdims=True) + jnp.sum(
        fresh_powers, axis=3, keepdims=True
    )
    cache_weights = (cache_powers / denominator).astype(jnp.bfloat16)
    fresh_weights = (fresh_powers / denominator).astype(jnp.bfloat16)
    mixture = jnp.einsum(
        "rgql,rlgd->rgqd", cache_weights, cached_values, preferred_element_type=jnp.float32
    )
    mixture = mixture + jnp.einsum(
        "rgqn,rngd->rgqd", fresh_weights, values_new, preferred_element_type=jnp.float32
    )
    return mixture.reshape(row_count, HEADS * HD).astype(jnp.bfloat16)


def local(
    hidden_in,
    norm_gain,
    query_weight,
    w_key,
    value_weight,
    w_output,
    paired_down_matrices,
    query_up_matrices,
    value_up_matrices,
    output_down_matrices,
    output_up_matrices,
    key_cache,
    value_cache,
    cache_lengths,
    row_adapter,
    old_slot,
    new_slot,
):
    instances = lax.axis_size("inst")
    tensor_ways = lax.axis_size("tp")
    resident = paired_down_matrices.shape[0]
    instance_index = lax.axis_index("inst")
    local_slots = jnp.arange(resident, dtype=jnp.int32)
    peer_ids = jnp.arange(instances, dtype=jnp.int32)
    leaving = owner_of(old_slot, instance_index * resident + local_slots)
    destination = lookup(new_slot, leaving) // resident
    send_routes = (destination[None, :] == peer_ids[:, None]).astype(jnp.bfloat16)
    arriving = owner_of(new_slot, instance_index * resident + local_slots)
    anchor = lookup(old_slot, arriving) // resident
    keep_routes = (anchor[:, None] == peer_ids[None, :]).astype(jnp.bfloat16)
    got_down, got_query_up, got_value_up, got_out_down, got_out_up = (
        lax.all_to_all(
            route_slots(paired_down_matrices, send_routes),
            "inst",
            split_axis=0,
            concat_axis=0,
            tiled=True,
        ),
        lax.all_to_all(
            route_slots(query_up_matrices, send_routes),
            "inst",
            split_axis=0,
            concat_axis=0,
            tiled=True,
        ),
        lax.all_to_all(
            route_slots(value_up_matrices, send_routes),
            "inst",
            split_axis=0,
            concat_axis=0,
            tiled=True,
        ),
        lax.all_to_all(
            route_slots(output_down_matrices, send_routes),
            "inst",
            split_axis=0,
            concat_axis=0,
            tiled=True,
        ),
        lax.all_to_all(
            route_slots(output_up_matrices, send_routes),
            "inst",
            split_axis=0,
            concat_axis=0,
            tiled=True,
        ),
    )
    store_down = route_slots(got_down, keep_routes)
    store_query_up = route_slots(got_query_up, keep_routes)
    store_value_up = route_slots(got_value_up, keep_routes)
    store_out_down = route_slots(got_out_down, keep_routes)
    store_out_up = route_slots(got_out_up, keep_routes)
    row_slot = lookup(new_slot, row_adapter) - instance_index * resident
    row_choice = row_slot[:, None] == local_slots[None, :]
    shard_width = hidden_in.shape[2]
    base_positions = cache_lengths.astype(jnp.float32)
    fresh_keys = []
    fresh_values = []
    collected_results = []
    for step_index in range(2):
        current = hidden_in[step_index]
        gathered, gain_whole = (
            lax.all_gather(current, "tp", axis=1, tiled=True),
            lax.all_gather(norm_gain.reshape(1, -1), "tp", axis=1, tiled=True),
        )
        values32 = gathered.astype(jnp.float32)
        scale_rows = lax.rsqrt(jnp.mean(values32 * values32, axis=1) + NORM_EPS)
        normed_whole = (values32 * scale_rows[:, None] * gain_whole.astype(jnp.float32)).astype(
            jnp.bfloat16
        )
        query_plain = jnp.dot(normed_whole, query_weight, preferred_element_type=jnp.float32)
        key_base = jnp.dot(normed_whole, w_key, preferred_element_type=jnp.float32)
        value_plain = jnp.dot(normed_whole, value_weight, preferred_element_type=jnp.float32)
        normed_part = lax.dynamic_slice_in_dim(
            normed_whole, lax.axis_index("tp") * shard_width, shard_width, 1
        )
        down_slots = jnp.einsum(
            "bs,hsi->hbi", normed_part, store_down, preferred_element_type=jnp.float32
        )
        rank_projection_input = lax.psum(select_slots(down_slots, row_choice), "tp").astype(
            jnp.bfloat16
        )
        query_delta = select_slots(
            jnp.einsum(
                "za,dao->dzo",
                rank_projection_input[:, :ADAPTER_RANK],
                store_query_up,
                preferred_element_type=jnp.float32,
            ),
            row_choice,
        )
        value_delta = select_slots(
            jnp.einsum(
                "za,dao->dzo",
                rank_projection_input[:, ADAPTER_RANK:],
                store_value_up,
                preferred_element_type=jnp.float32,
            ),
            row_choice,
        )
        query_updated = (query_plain + ADAPTER_SCALING * query_delta).astype(jnp.bfloat16)
        key_new = key_base.astype(jnp.bfloat16)
        value_updated = (value_plain + ADAPTER_SCALING * value_delta).astype(jnp.bfloat16)
        query_rows, paired_rows = (
            lax.all_to_all(query_updated, "tp", split_axis=0, concat_axis=1, tiled=True),
            lax.all_to_all(
                jnp.concatenate([key_new, value_updated], axis=1),
                "tp",
                split_axis=0,
                concat_axis=1,
                tiled=True,
            ),
        )
        own_rows = query_rows.shape[0]
        paired = paired_rows.reshape(own_rows, tensor_ways, 2, key_new.shape[1])
        keys_rows = paired[:, :, 0, :].reshape(own_rows, KV_HEADS, HD)
        values_rows = paired[:, :, 1, :].reshape(own_rows, KV_HEADS, HD)
        positions = base_positions + step_index
        query_rot = rotary(
            query_rows.astype(jnp.float32).reshape(own_rows, HEADS, HD), positions
        ).astype(jnp.bfloat16)
        key_rot = rotary(keys_rows.astype(jnp.float32), positions).astype(jnp.bfloat16)
        fresh_keys.append(key_rot)
        fresh_values.append(values_rows)
        attention_result = attend_rows(
            query_rot,
            jnp.stack(fresh_keys, axis=1),
            jnp.stack(fresh_values, axis=1),
            key_cache,
            value_cache,
            cache_lengths,
        )
        attended_heads = lax.all_to_all(
            attention_result, "tp", split_axis=1, concat_axis=0, tiled=True
        )
        out_slots = jnp.einsum(
            "uv,xlv->xul", attended_heads, store_out_down, preferred_element_type=jnp.float32
        )
        output_rank_vectors = lax.psum(
            select_slots(out_slots, row_choice).astype(jnp.bfloat16), "tp"
        )
        output_delta = select_slots(
            jnp.einsum(
                "us,gsy->guy", output_rank_vectors, store_out_up, preferred_element_type=jnp.float32
            ),
            row_choice,
        )
        base_projection_output = lax.psum_scatter(
            lax.dot_general(
                w_output,
                attended_heads,
                (((0,), (1,)), ((), ())),
                preferred_element_type=jnp.float32,
            ),
            "tp",
            scatter_dimension=0,
            tiled=True,
        )
        collected_results.append(
            (jnp.transpose(base_projection_output) + ADAPTER_SCALING * output_delta).astype(
                jnp.bfloat16
            )
        )
    return jnp.stack(collected_results, axis=0)


def solution(mesh):
    placed = (
        P(None, "inst", "tp"),
        P("tp"),
        P(None, "tp"),
        P(None, "tp"),
        P(None, "tp"),
        P("tp", None),
        P("inst", "tp", None),
        P("inst", None, "tp"),
        P("inst", None, "tp"),
        P("inst", None, "tp"),
        P("inst", None, "tp"),
        P(("inst", "tp"), None, None),
        P(("inst", "tp"), None, None),
        P(("inst", "tp")),
        P("inst"),
        P(),
        P(),
    )
    return jax.shard_map(
        local, mesh=mesh, in_specs=placed, out_specs=P(None, "inst", "tp"), check_vma=False
    )
```

profile of v0, /device:TPU:2, one launch (start us, length us, event | category | flops | bytes accessed | tf_op | source)
XLA Modules:
  0.0 458.0 jit_solution(8227292135772625393)
XLA Ops:
  6.5 1.8 fusion.125
  8.3 0.8 select_reduce_fusion.6
  9.2 0.9 select_reduce_fusion.5
  10.0 0.8 select_reduce_fusion.3
  10.9 1.1 convolution_convert_fusion.7
  12.1 0.8 reshape.414
  12.8 8.6 %all-to-all-start.3 = ((bf16[16,2,1024]{2,1,0:T(2,128)(2,1)}), bf16[16,2,1024]{2,1,0:T(2,128)(2,1)S(1)}, u32[]{:S(2)}, u32[]{:S(2)}) async-start(bf16[16,2,1024]{2,1,0:T(2,128)(2,1)} %reshape.414), calls=%async_computation.3 | async-start | bytes 131072 | tf_op jit(solution)/shard_map/all_to_all | solution.py:140
  21.4 1.4 convolution_convert_fusion.4
  22.8 1.0 copy.190
  23.8 5.5 %all-to-all-done.3 = bf16[16,2,1024]{2,1,0:T(2,128)(2,1)S(1)} async-done(((bf16[16,2,1024]{2,1,0:T(2,128)(2,1)}), bf16[16,2,1024]{2,1,0:T(2,128)(2,1)S(1)}, u32[]{:S(2)}, u32[]{:S(2)}) %all-to-all-start.3) | async-done | bytes 65568 | tf_op jit(solution)/shard_map/all_to_all | solution.py:140
  29.3 3.6 all-to-all-start
  32.9 0.7 all-gather.9.cloned.1.call-update
  33.6 1.0 convolution_convert_fusion
  34.7 1.9 copy.193
  36.6 12.2 %all-to-all-done = bf16[16,64,256]{2,1,0:T(8,128)(2,1)S(1)} async-done(((bf16[16,64,256]{2,1,0:T(8,128)(2,1)}), bf16[16,64,256]{2,1,0:T(8,128)(2,1)S(1)}, u32[]{:S(2)}, u32[]{:S(2)}) %all-to-all-start) | async-done | bytes 524320 | tf_op jit(solution)/shard_map/all_to_all | solution.py:133
  48.8 0.8 copy-done.6
  49.6 4.2 all-to-all-start.1
  53.9 23.3 %all-gather.3 = bf16[16,1,512]{2,1,0:T(2,128)(2,1)S(1)} all-gather(bf16[1,1,512]{2,1,0:T(2,128)(2,1)S(1)} %reshape.397), channel_id=3, replica_groups=mesh['inst'=16,'tp'=16] {'tp'}, dimensions={0}, use_global_device_ids=true | all-gather | bytes 17408 | tf_op jit(solution)/shard_map/all_gather | solution.py:178
  78.1 0.7 multiply_cosine_fusion.1
  79.2 1.5 convolution_convert_fusion.6
  80.7 2.1 fusion
  82.7 37.0 %all-gather.9.cloned.1.call-done = bf16[1,128,8192]{2,1,0:T(8,128)(2,1)} async-done(((bf16[1,128,512]{2,1,0:T(8,128)(2,1)}), bf16[1,128,8192]{2,1,0:T(8,128)(2,1)}) %all-gather.9.cloned.1.call-update) | async-done | bytes 2097168 | tf_op jit(solution)/shard_map/all_gather | solution.py:177
  119.7 2.1 fusion.3
  121.8 2.3 fusion.8
  124.1 2.4 copy.195
  126.6 3.4 fusion.2
  130.0 1.1 fusion.13
  131.1 1.1 fusion.14
  132.1 0.8 convolution_convert_fusion.9
  133.0 1.4 convolution_convert_fusion.10
  134.4 67.8 %all-reduce.3 = (bf16[128,128]{0,1:T(8,128)(2,1)S(1)}, bf16[128,128]{0,1:T(8,128)(2,1)S(1)}) all-reduce(f32[128,128]{0,1:T(8,128)} %bitcast.210, f32[128,128]{0,1:T(8,128)} %bitcast.211), channel_id=1, replica_groups=mesh['inst'=16,'tp'=16] {'tp'}, use_global_device_ids=true, to_apply=%region_7.8 | all-reduce | flops 32768 | bytes 196608 | tf_op jit(solution)/shard_map/psum | solution.py:194
  202.8 0.7 fusion.23
  203.5 1.1 fusion.11
  204.6 1.7 fusion.12
  206.3 0.8 fusion.28
  207.3 0.7 reshape.418
  208.0 9.9 %all-to-all-start.9 = ((bf16[16,2,256]{2,1,0:T(2,128)(2,1)}), bf16[16,2,256]{2,1,0:T(2,128)(2,1)S(1)}, u32[]{:S(2)}, u32[]{:S(2)}) async-start(bf16[16,2,256]{2,1,0:T(2,128)(2,1)} %reshape.418), calls=%async_computation.10 | async-start | bytes 32768 | tf_op jit(solution)/shard_map/all_to_all | solution.py:220
  217.9 3.1 fusion.27
  221.1 1.0 copy.220
  222.1 4.3 fusion.26
  226.5 1.4 fusion.25
  228.0 0.7 reshape.416
  228.7 7.3 %all-to-all-start.4 = ((bf16[16,2,256]{2,1,0:T(2,128)(2,1)}), bf16[16,2,256]{2,1,0:T(2,128)(2,1)S(1)}, u32[]{:S(2)}, u32[]{:S(2)}) async-start(bf16[16,2,256]{2,1,0:T(2,128)(2,1)} %reshape.416), calls=%async_computation.4 | async-start | bytes 32768 | tf_op jit(solution)/shard_map/all_to_all | solution.py:220
  236.4 5.8 %all-to-all-done.4 = bf16[16,2,256]{2,1,0:T(2,128)(2,1)S(1)} async-done(((bf16[16,2,256]{2,1,0:T(2,128)(2,1)}), bf16[16,2,256]{2,1,0:T(2,128)(2,1)S(1)}, u32[]{:S(2)}, u32[]{:S(2)}) %all-to-all-start.4) | async-done | bytes 16416 | tf_op jit(solution)/shard_map/all_to_all | solution.py:220
  242.2 4.8 %all-to-all-start.2 = ((bf16[16,8,256]{2,1,0:T(8,128)(2,1)}), bf16[16,8,256]{2,1,0:T(8,128)(2,1)S(1)}, u32[]{:S(2)}, u32[]{:S(2)}) async-start(bf16[16,8,256]{2,1,0:T(8,128)(2,1)} %fusion.26), calls=%async_computation.2 | async-start | bytes 131072 | tf_op jit(solution)/shard_map/all_to_all | solution.py:219
  247.9 5.4 %all-to-all-done.2 = bf16[16,8,256]{2,1,0:T(8,128)(2,1)S(1)} async-done(((bf16[16,8,256]{2,1,0:T(8,128)(2,1)}), bf16[16,8,256]{2,1,0:T(8,128)(2,1)S(1)}, u32[]{:S(2)}, u32[]{:S(2)}) %all-to-all-start.2) | async-done | bytes 65568 | tf_op jit(solution)/shard_map/all_to_all | solution.py:219
  253.3 4.8 %all-to-all-start.8 = ((bf16[16,8,256]{2,1,0:T(8,128)(2,1)}), bf16[16,8,256]{2,1,0:T(8,128)(2,1)S(1)}, u32[]{:S(2)}, u32[]{:S(2)}) async-start(bf16[16,8,256]{2,1,0:T(8,128)(2,1)} %fusion.25), calls=%async_computation.9 | async-start | bytes 131072 | tf_op jit(solution)/shard_map/all_to_all | solution.py:219
  258.3 6.1 %all-to-all-done.8 = bf16[16,8,256]{2,1,0:T(8,128)(2,1)S(1)} async-done(((bf16[16,8,256]{2,1,0:T(8,128)(2,1)}), bf16[16,8,256]{2,1,0:T(8,128)(2,1)S(1)}, u32[]{:S(2)}, u32[]{:S(2)}) %all-to-all-start.8) | async-done | bytes 65568 | tf_op jit(solution)/shard_map/all_to_all | solution.py:219
  266.5 10.9 %all_to_all.115 = bf16[8,16,256]{2,0,1:T(8,128)(2,1)S(1)} all-to-all(bf16[8,16,256]{2,0,1:T(8,128)(2,1)S(1)} %copy.238), channel_id=1, replica_groups=mesh['inst'=16,'tp'=16] {'tp'}, dimensions={1} | all-to-all | bytes 131072 | tf_op jit(solution)/shard_map/all_to_all | solution.py:247
  277.4 4.8 %convolution_bitcast_fusion = f32[8192,128]{0,1:T(8,128)} fusion(bf16[256,8192]{1,0:T(8,128)(2,1)} %param.22, bf16[8,16,256]{2,0,1:T(8,128)(2,1)S(1)} %all_to_all.115), kind=kOutput, calls=%fused_computation | convolution fusion | flops 536870912 | bytes 8454144 | tf_op jit(solution)/shard_map/dot_general | solution.py:263
  283.9 10.9 %all_to_all.116 = bf16[8,16,256]{2,0,1:T(8,128)(2,1)S(1)} all-to-all(bf16[8,16,256]{2,0,1:T(8,128)(2,1)S(1)} %copy.208), channel_id=1, replica_groups=mesh['inst'=16,'tp'=16] {'tp'}, dimensions={1} | all-to-all | bytes 131072 | tf_op jit(solution)/shard_map/all_to_all | solution.py:247
  294.8 4.9 %convolution_bitcast_fusion.1 = f32[8192,128]{0,1:T(8,128)} fusion(bf16[256,8192]{1,0:T(8,128)(2,1)} %param.22, bf16[8,16,256]{2,0,1:T(8,128)(2,1)S(1)} %all_to_all.116), kind=kOutput, calls=%fused_computation.1 | convolution fusion | flops 536870912 | bytes 8454144 | tf_op jit(solution)/shard_map/dot_general | solution.py:263
  299.7 0.9 copy-done.9
  301.0 1.0 copy.213
  302.0 7.1 %all-to-all-start.7 = ((bf16[16,64,256]{2,1,0:T(8,128)(2,1)}), bf16[16,64,256]{2,1,0:T(8,128)(2,1)S(1)}, u32[]{:S(2)}, u32[]{:S(2)}) async-start(bf16[16,64,256]{2,1,0:T(8,128)(2,1)} %copy.213), calls=%async_computation.8 | async-start | bytes 1048576 | tf_op jit(solution)/shard_map/all_to_all | solution.py:147
  309.7 1.6 copy.210
  311.4 13.8 %all-to-all-done.7 = bf16[16,64,256]{2,1,0:T(8,128)(2,1)S(1)} async-done(((bf16[16,64,256]{2,1,0:T(8,128)(2,1)}), bf16[16,64,256]{2,1,0:T(8,128)(2,1)S(1)}, u32[]{:S(2)}, u32[]{:S(2)}) %all-to-all-start.7) | async-done | bytes 524320 | tf_op jit(solution)/shard_map/all_to_all | solution.py:147
  325.1 4.2 all-to-all-start.6
  329.7 26.2 %all-to-all-done.6 = bf16[16,64,512]{2,1,0:T(8,128)(2,1)S(1)} async-done(((bf16[16,64,512]{2,1,0:T(8,128)(2,1)}), bf16[16,64,512]{2,1,0:T(8,128)(2,1)S(1)}, u32[]{:S(2)}, u32[]{:S(2)}) %all-to-all-start.6) | async-done | bytes 1048608 | tf_op jit(solution)/shard_map/all_to_all | solution.py:154
  357.2 66.3 %all-reduce.1 = (bf16[128,64]{0,1:T(8,128)(2,1)S(1)}, bf16[128,64]{0,1:T(8,128)(2,1)S(1)}) all-reduce(bf16[128,64]{0,1:T(8,128)(2,1)S(1)} %bitcast.212, bf16[128,64]{0,1:T(8,128)(2,1)S(1)} %bitcast.213), channel_id=1, replica_groups=mesh['inst'=16,'tp'=16] {'tp'}, use_global_device_ids=true, to_apply=%region_27.28 | all-reduce | flops 16384 | bytes 65536 | tf_op jit(solution)/shard_map/psum | solution.py:253
  424.8 1.0 fusion.51
  425.8 23.9 %reduce-scatter.3.cloned.1.call-done = f32[512,128]{0,1:T(8,128)} async-done(((f32[8192,128]{0,1:T(8,128)}), f32[512,128]{0,1:T(8,128)}) %reduce-scatter.3.cloned.1.call-update) | async-done | bytes 262160 | tf_op jit(solution)/shard_map/reduce_scatter | solution.py:262
  449.7 1.0 fusion.50
  450.7 0.7 pad_maximum_fusion
  (151 shorter events, 11.1 us)
Async XLA Ops:
  6.5 27.1 %copy-start = (bf16[8,512,128]{2,1,0:T(8,128)(2,1)S(1)}, bf16[8,512,128]{2,1,0:T(8,128)(2,1)}, u32[]{:S(2)}) copy-start(bf16[8,512,128]{2,1,0:T(8,128)(2,1)} %param.23) | copy-start | bytes 3145732
  6.5 74.1 %all-gather.7.cloned.1.call-start = ((), (), s32[]{:S(2)}) async-start(), calls=%async_computation.15 | async-start | bytes 2228224 | tf_op jit(solution)/shard_map/all_gather | solution.py:177
  10.9 23.8 %copy-start.17 = (s32[8]{0:T(128)}, s32[8]{0:T(128)S(1)}, u32[]{:S(2)}) copy-start(s32[8]{0:T(128)S(1)} %and_select_fusion) | copy-start | bytes 100
  12.8 16.4 %all-to-all-start.3 = ((bf16[16,2,1024]{2,1,0:T(2,128)(2,1)}), bf16[16,2,1024]{2,1,0:T(2,128)(2,1)S(1)}, u32[]{:S(2)}, u32[]{:S(2)}) async-start(bf16[16,2,1024]{2,1,0:T(2,128)(2,1)} %reshape.414), calls=%async_computation.3 | async-start | bytes 131072 | tf_op jit(solution)/shard_map/all_to_all | solution.py:140
  29.3 19.5 %all-to-all-start = ((bf16[16,64,256]{2,1,0:T(8,128)(2,1)}), bf16[16,64,256]{2,1,0:T(8,128)(2,1)S(1)}, u32[]{:S(2)}, u32[]{:S(2)}) async-start(bf16[16,64,256]{2,1,0:T(8,128)(2,1)} %copy.190), calls=%async_computation | async-start | bytes 1048576 | tf_op jit(solution)/shard_map/all_to_all | solution.py:133
  32.9 86.9 %all-gather.9.cloned.1.call-start = ((), (), s32[]{:S(2)}) async-start(), calls=%async_computation.16 | async-start | bytes 2228224 | tf_op jit(solution)/shard_map/all_gather | solution.py:177
  36.5 17.3 %copy-start.28 = (s32[8]{0:T(128)S(1)}, s32[8]{0:T(128)}, u32[]{:S(2)}) copy-start(s32[8]{0:T(128)} %param.30) | copy-start | bytes 100
  36.5 17.3 %copy-start.22 = (bf16[512]{0:T(512)(128)(2,1)S(1)}, bf16[512]{0:T(512)(128)(2,1)}, u32[]{:S(2)}) copy-start(bf16[512]{0:T(512)(128)(2,1)} %param.18) | copy-start | bytes 3076
  36.5 40.7 %copy-start.26 = (s32[128]{0:T(128)S(1)}, s32[128]{0:T(128)}, u32[]{:S(2)}) copy-start(s32[128]{0:T(128)} %param.33) | copy-start | bytes 1540
  36.6 40.7 %copy-start.27 = (s32[128]{0:T(128)S(1)}, s32[128]{0:T(128)}, u32[]{:S(2)}) copy-start(s32[128]{0:T(128)} %param.31) | copy-start | bytes 1540
  48.8 0.8 copy-start.6
  49.6 72.2 %all-to-all-start.1 = ((bf16[16,512,128]{2,1,0:T(8,128)(2,1)}), bf16[16,512,128]{2,1,0:T(8,128)(2,1)S(1)}, u32[]{:S(2)}, u32[]{:S(2)}) async-start(bf16[16,512,128]{2,1,0:T(8,128)(2,1)} %copy.193), calls=%async_computation.1 | async-start | bytes 4194304 | tf_op jit(solution)/shard_map/all_to_all | solution.py:126
  77.5 44.3 %copy-start.19 = (s32[8]{0:T(128)}, s32[8]{0:T(128)S(1)}, u32[]{:S(2)}) copy-start(s32[8]{0:T(128)S(1)} %and_select_fusion.1) | copy-start | bytes 100
  78.1 126.5 %copy-start.29 = (pred[8,128]{1,0:T(8,128)(4,1)}, pred[8,128]{1,0:T(8,128)(4,1)S(1)}, u32[]{:S(2)}) copy-start(pred[8,128]{1,0:T(8,128)(4,1)S(1)} %iota_compare_fusion.5) | copy-start | bytes 3076
  126.6 3.4 copy-start.7
  130.0 3.0 copy-start.1
  130.0 2.2 copy-start.3
  202.2 0.6 copy-start.24
  202.2 0.6 copy-start.25
  202.2 4.2 copy-start.4
  206.3 11.6 %copy-start.16 = (f32[32,128]{1,0:T(8,128)S(1)}, f32[32,128]{1,0:T(8,128)}, u32[]{:S(2)}) copy-start(f32[32,128]{1,0:T(8,128)} %fusion.23) | copy-start | bytes 49156
  208.0 20.7 %all-to-all-start.9 = ((bf16[16,2,256]{2,1,0:T(2,128)(2,1)}), bf16[16,2,256]{2,1,0:T(2,128)(2,1)S(1)}, u32[]{:S(2)}, u32[]{:S(2)}) async-start(bf16[16,2,256]{2,1,0:T(2,128)(2,1)} %reshape.418), calls=%async_computation.10 | async-start | bytes 32768 | tf_op jit(solution)/shard_map/all_to_all | solution.py:220
  222.1 4.3 copy-start.2
  226.5 1.4 copy-start.14
  226.5 1.4 copy-start.15
  226.5 20.9 %copy-start.12 = (f32[8,64]{1,0:T(8,128)S(1)}, f32[8,64]{1,0:T(8,128)}, u32[]{:S(2)}) copy-start(f32[8,64]{1,0:T(8,128)} %get-tuple-element.33) | copy-start | bytes 6148
  226.5 21.0 %copy-start.13 = (f32[8,64]{1,0:T(8,128)S(1)}, f32[8,64]{1,0:T(8,128)}, u32[]{:S(2)}) copy-start(f32[8,64]{1,0:T(8,128)} %get-tuple-element.34) | copy-start | bytes 6148
  226.5 21.0 %copy-start.10 = (f32[8,64]{1,0:T(8,128)S(1)}, f32[8,64]{1,0:T(8,128)}, u32[]{:S(2)}) copy-start(f32[8,64]{1,0:T(8,128)} %get-tuple-element.29) | copy-start | bytes 6148
  226.5 21.0 %copy-start.11 = (f32[8,64]{1,0:T(8,128)S(1)}, f32[8,64]{1,0:T(8,128)}, u32[]{:S(2)}) copy-start(f32[8,64]{1,0:T(8,128)} %get-tuple-element.30) | copy-start | bytes 6148
  228.7 13.5 %all-to-all-start.4 = ((bf16[16,2,256]{2,1,0:T(2,128)(2,1)}), bf16[16,2,256]{2,1,0:T(2,128)(2,1)S(1)}, u32[]{:S(2)}, u32[]{:S(2)}) async-start(bf16[16,2,256]{2,1,0:T(2,128)(2,1)} %reshape.416), calls=%async_computation.4 | async-start | bytes 32768 | tf_op jit(solution)/shard_map/all_to_all | solution.py:220
  236.2 28.5 %copy-start.5 = (bf16[8,64,512]{2,1,0:T(8,128)(2,1)S(1)}, bf16[8,64,512]{2,1,0:T(8,128)(2,1)}, u32[]{:S(2)}) copy-start(bf16[8,64,512]{2,1,0:T(8,128)(2,1)} %param.28) | copy-start | bytes 1572868
  236.2 28.5 %copy-start.21 = (pred[8,64]{1,0:T(8,128)(4,1)S(1)}, pred[8,64]{1,0:T(8,128)(4,1)}, u32[]{:S(2)}) copy-start(pred[8,64]{1,0:T(8,128)(4,1)} %iota_compare_fusion.6) | copy-start | bytes 1540
  242.2 11.1 %all-to-all-start.2 = ((bf16[16,8,256]{2,1,0:T(8,128)(2,1)}), bf16[16,8,256]{2,1,0:T(8,128)(2,1)S(1)}, u32[]{:S(2)}, u32[]{:S(2)}) async-start(bf16[16,8,256]{2,1,0:T(8,128)(2,1)} %fusion.26), calls=%async_computation.2 | async-start | bytes 131072 | tf_op jit(solution)/shard_map/all_to_all | solution.py:219
  253.3 11.1 %all-to-all-start.8 = ((bf16[16,8,256]{2,1,0:T(8,128)(2,1)}), bf16[16,8,256]{2,1,0:T(8,128)(2,1)S(1)}, u32[]{:S(2)}, u32[]{:S(2)}) async-start(bf16[16,8,256]{2,1,0:T(8,128)(2,1)} %fusion.25), calls=%async_computation.9 | async-start | bytes 131072 | tf_op jit(solution)/shard_map/all_to_all | solution.py:219
  258.2 166.7 %reduce-scatter.5.cloned.1.call-start = ((), (), s32[]{:S(2)}) async-start(), calls=%async_computation.14 | async-start | bytes 4456448 | tf_op jit(solution)/shard_map/reduce_scatter | solution.py:262
  258.2 7.8 %copy-start.23 = (bf16[8,64,512]{2,1,0:T(8,128)(2,1)S(1)}, bf16[8,64,512]{2,1,0:T(8,128)(2,1)}, u32[]{:S(2)}) copy-start(bf16[8,64,512]{2,1,0:T(8,128)(2,1)} %param.29) | copy-start | bytes 1572868
  282.2 167.5 %reduce-scatter.3.cloned.1.call-start = ((), (), s32[]{:S(2)}) async-start(), calls=%async_computation.13 | async-start | bytes 4456448 | tf_op jit(solution)/shard_map/reduce_scatter | solution.py:262
  299.6 0.9 copy-start.9
  299.7 1.0 copy-start.18
  300.6 8.5 %copy-start.8 = (bf16[8,64,512]{2,1,0:T(8,128)(2,1)S(1)}, bf16[8,64,512]{2,1,0:T(8,128)(2,1)}, u32[]{:S(2)}) copy-start(bf16[8,64,512]{2,1,0:T(8,128)(2,1)} %param.27) | copy-start | bytes 1572868
  302.0 23.2 %all-to-all-start.7 = ((bf16[16,64,256]{2,1,0:T(8,128)(2,1)}), bf16[16,64,256]{2,1,0:T(8,128)(2,1)S(1)}, u32[]{:S(2)}, u32[]{:S(2)}) async-start(bf16[16,64,256]{2,1,0:T(8,128)(2,1)} %copy.213), calls=%async_computation.8 | async-start | bytes 1048576 | tf_op jit(solution)/shard_map/all_to_all | solution.py:147
  309.7 19.6 %copy-start.20 = (s32[8]{0:T(128)S(1)}, s32[8]{0:T(128)}, u32[]{:S(2)}) copy-start(s32[8]{0:T(128)} %copy-done.19) | copy-start | bytes 100
  311.4 45.3 %copy-start.30 = (pred[8,128]{1,0:T(8,128)(4,1)S(1)}, pred[8,128]{1,0:T(8,128)(4,1)}, u32[]{:S(2)}) copy-start(pred[8,128]{1,0:T(8,128)(4,1)} %copy-done.29) | copy-start | bytes 3076
  325.1 30.8 %all-to-all-start.6 = ((bf16[16,64,512]{2,1,0:T(8,128)(2,1)}), bf16[16,64,512]{2,1,0:T(8,128)(2,1)S(1)}, u32[]{:S(2)}, u32[]{:S(2)}) async-start(bf16[16,64,512]{2,1,0:T(8,128)(2,1)} %copy.210), calls=%async_computation.7 | async-start | bytes 2097152 | tf_op jit(solution)/shard_map/all_to_all | solution.py:154
Sparse Core Ops, SparseCore 0:
  9.8 55.3 all-gather.6
  67.5 52.1 all-gather.8
  282.4 81.2 reduce-scatter.4
  367.6 82.1 reduce-scatter.2
where the time goes:
time: 459 us; the launch traced here: 458 us
  blocking collectives  179 us (39%)
  waiting for transfers between devices  137 us (30%)
  starting transfers between devices  54.6 us (12%)
  matrix products  40.8 us (9%)
  local copies, waits for them, and re-layouts  17.2 us (4%)
  other arithmetic  15.4 us (3%)
  between operations  13.9 us (3%)
    psum x1, blocking collectives, local(): lax.psum(select_slots(down_slots, row_choice), 'tp').astype(jnp.bfloat16)  67.8 us
    psum x1, blocking collectives, local(): lax.psum(select_slots(out_slots, row_choice).astype(jnp.bfloat16), 'tp')  66.3 us
    all_gather x2, waiting for transfers between devices, local(): lax.all_gather(current, 'tp', axis=1, tiled=True)  37 us
    all_to_all x1, waiting for transfers between devices, local(): lax.all_to_all(route_slots(output_up_matrices, send_routes), 'inst', spli...  26.2 us
    reduce_scatter x2, waiting for transfers between devices, local(): lax.psum_scatter(lax.dot_general(w_output, attended_heads, (((0,), (1,)),...  23.9 us
    all_gather x1, blocking collectives, local(): lax.all_gather(norm_gain.reshape(1, -1), 'tp', axis=1, tiled=True)  23.3 us
    all_to_all x2, blocking collectives, local(): lax.all_to_all(attention_result, 'tp', split_axis=1, concat_axis=0, tiled...  21.8 us
    all_to_all x2, starting transfers between devices, local(): lax.all_to_all(jnp.concatenate([key_new, value_updated], axis=1), 'tp', s...  17.2 us
  transfers between devices with their start and end apart: 13, of which 9 were waited for; matrix products, arithmetic and copies ran while one was open for 9% of the time, Pallas kernels for 0%

commit v1 on v0

v1 whole, which is shorter than its diff:
```python
import functools
import math

import jax
import jax.numpy as jnp
from jax import lax
from jax.experimental import pallas as pl
from jax.experimental.pallas import tpu as pltpu
from jax.sharding import PartitionSpec as P

MESH = pl.DeviceIdType.MESH
F32, BF16 = jnp.float32, jnp.bfloat16

NT = 16
NI = 16
SIDE = 4
D = 8192
SH = 512
ROWS = 128
R2 = 256
OWN = 16
HEADS = 32
HD = 128
SLOTS = 8
LMAX = 64
LPAD = 80
ADAPTER_SCALING = 0.5
NORM_EPS = 1e-05
ROPE_BASE = 500000.0

SCRATCH = dict(
    hidv=((2, ROWS, SH), BF16),
    ag=((NT, R2, SH), BF16),
    wqv=((D, 256), BF16),
    wkv=((256, D), BF16),
    wof=((NT, 2, 128, SH), BF16),
    dnv=((SLOTS, SH, 128), BF16),
    quv=((SLOTS, 64, 256), BF16),
    vuv=((SLOTS, 32, 64), BF16),
    odv=((SLOTS, 64, 256), BF16),
    ouv=((SLOTS, 64, SH), BF16),
    dns=((NI, SH, 128), BF16),
    qus=((NI, 64, 256), BF16),
    vus=((NI, 32, 128), BF16),
    ods=((NI, 64, 256), BF16),
    ous=((NI, 64, SH), BF16),
    dnr=((NI, SH, 128), BF16),
    qur=((NI, 64, 256), BF16),
    vur=((NI, 32, 128), BF16),
    odr=((NI, 64, 256), BF16),
    our=((NI, 64, SH), BF16),
    qcat=((SLOTS * 128, 256), BF16),
    vcat=((128, SLOTS * 128), BF16),
    oucat=((SLOTS * 128, SH), BF16),
    rall=((R2, SLOTS * 128), BF16),
    rall2=((R2, SLOTS * 128), BF16),
    kext=((8, LPAD, 512), BF16),
    vext=((8, LPAD, 512), BF16),
    ssb=((NT, 8, 128), F32),
    rs1s=((NT, OWN, 128), F32),
    rs1r=((NT, OWN, 128), F32),
    rk1=((NT, OWN, 128), BF16),
    rs2s=((NT, OWN, 128), F32),
    rs2r=((NT, OWN, 128), F32),
    rk2=((NT, OWN, 128), BF16),
    qacc=((R2, 256), F32),
    kvacc=((R2, 256), F32),
    qkvs=((NT, OWN, 512), BF16),
    qkvr=((NT, OWN, 512), BF16),
    q2=((OWN * HEADS, HD), F32),
    o2=((OWN * HEADS, HD), F32),
    ag2=((NT, OWN, HEADS * HD), BF16),
    attd=((NT, OWN, 256), BF16),
    oacc=((R2, SH), F32),
)
SEMS = dict(
    ld=(16,),
    ss_s=(NT,), ss_r=(NT,),
    ag_s=(2, 20), ag_r=(2, NT, 2),
    z_s=(5, NI), z_r=(5, NI),
    wo_s=(NT,), wo_r=(NT,), sib_s=(1,), sib_r=(1,),
    rs1_s=(NT,), rs1_r=(NT,), rk1_s=(NT,), rk1_r=(NT,),
    qkv_s=(NT,), qkv_r=(NT,),
    ag2_s=(2, 20), ag2_r=(2, NT, 2),
    at_s=(NT,), at_r=(NT,),
    rs2_s=(NT,), rs2_r=(NT,), rk2_s=(NT,), rk2_r=(NT,),
)
INPUTS = (
    "tabs", "lens", "gain", "rmask", "hid", "wq", "wk", "wv", "wo",
    "dn", "qu", "vu", "od", "ou", "kc", "vc",
)


class Refs:
    pass


def dot(a, b):
    return lax.dot_general(a, b, (((1,), (0,)), ((), ())), preferred_element_type=F32)


def dot_nt(a, b):
    return lax.dot_general(a, b, (((1,), (1,)), ((), ())), preferred_element_type=F32)


def remote(src, dst, ssem, rsem, **where):
    return pltpu.make_async_remote_copy(
        src_ref=src, dst_ref=dst, send_sem=ssem, recv_sem=rsem, device_id=where, device_id_type=MESH
    )


def loop(lo, hi, body):
    lax.fori_loop(lo, hi, lambda k, c: (body(k), c)[1], 0)


def peers(me, n, body):
    loop(1, n, lambda k: body(lax.rem(me + k, n)))


def mesh_gather(x, y, ref_of, ssem, rsem):
    def at(p, da, db):
        ax, ay = (da, db) if p == 0 else (db, da)
        return lax.rem(x + ax + SIDE, SIDE) * SIDE + lax.rem(y + ay + SIDE, SIDE)

    count = [0, 0]
    sent = []

    def copy(p, da, db, half, to, idx):
        block = at(p, da, db)
        ref = ref_of(block, p, half)
        return remote(
            ref, ref, ssem.at[p, idx], rsem.at[p, block, half or 0], tp=at(p, *to)
        )

    def send(p, da, db, half, to):
        c = copy(p, da, db, half, to, count[p])
        count[p] += 1
        c.start()
        sent.append(c)

    def wait(p, da, db, half=None):
        copy(p, da, db, half, (1, 0), 0).wait_recv()

    def start():
        for p in range(2):
            for to in ((1, 0), (-1, 0), (0, 1), (0, -1)):
                send(p, 0, 0, None, to)

    def along_b(p, da):
        send(p, da, 0, None, (0, 1))
        send(p, da, 0, None, (0, -1))

    def s1():
        for p in range(2):
            wait(p, -1, 0)
            send(p, -1, 0, 0, (1, 0))
            along_b(p, -1)
        for p in range(2):
            wait(p, 1, 0)
            send(p, 1, 0, 1, (-1, 0))
            along_b(p, 1)

    def s2():
        for p in range(2):
            wait(p, 0, -1)
            send(p, 0, -1, 0, (0, 1))
            wait(p, 0, 1)
            send(p, 0, 1, 1, (0, -1))

    def s3():
        for p in range(2):
            wait(p, 2, 0, 0)
            wait(p, 2, 0, 1)
            along_b(p, 2)

    def s4():
        for da in (-1, 1):
            for p in range(2):
                wait(p, da, -1)
                send(p, da, -1, 0, (0, 1))
                wait(p, da, 1)
                send(p, da, 1, 1, (0, -1))

    def s5():
        for p in range(2):
            wait(p, 0, 2, 0)
            wait(p, 0, 2, 1)

    def s6():
        for p in range(2):
            wait(p, 2, -1)
            send(p, 2, -1, 0, (0, 1))
            wait(p, 2, 1)
            send(p, 2, 1, 1, (0, -1))

    def s7():
        for da in (-1, 1, 2):
            for p in range(2):
                wait(p, da, 2, 0)
                wait(p, da, 2, 1)

    return start, (s1, s2, s3, s4, s5, s6, s7), sent


def kernel(*args):
    names = list(INPUTS) + ["out"] + list(SCRATCH) + list(SEMS)
    r = Refs()
    for name, ref in zip(names, args, strict=True):
        setattr(r, name, ref)
    i = lax.axis_index("inst")
    t = lax.axis_index("tp")
    x, y = t // SIDE, lax.rem(t, SIDE)
    core = lax.rem(i, 2)
    sibling = i + 1 - 2 * core

    loads = {}

    def load(name, src, dst):
        c = pltpu.make_async_copy(src, dst, r.ld.at[len(loads)])
        c.start()
        loads[name] = c

    load("hid", r.hid, r.hidv)
    for m in ("dn", "qu", "vu", "od", "ou"):
        load(m, getattr(r, m), getattr(r, m + "v"))

    bar = pltpu.get_barrier_semaphore()

    def hello(axis, p):
        pl.semaphore_signal(bar, inc=1, device_id={axis: p}, device_id_type=MESH)

    peers(t, NT, lambda p: hello("tp", p))
    peers(i, NI, lambda p: hello("inst", p))

    eye = lax.broadcasted_iota(jnp.int32, (128, 128), 0) == lax.broadcasted_iota(
        jnp.int32, (128, 128), 1
    )
    loads["hid"].wait()
    parts = []
    for s in range(2):
        h = r.hidv[s].astype(F32)
        column = jnp.sum(h * h, axis=1, keepdims=True)
        parts.append(jnp.sum(jnp.where(eye, column, 0.0), axis=0, keepdims=True))
    r.ssb[t] = jnp.concatenate(parts + [jnp.zeros((6, 128), F32)], axis=0)

    pl.semaphore_wait(bar, NT + NI - 2)

    def ss_copy(src_block, to):
        return remote(
            r.ssb.at[src_block], r.ssb.at[src_block], r.ss_s.at[to], r.ss_r.at[src_block], tp=to
        )

    peers(t, NT, lambda p: ss_copy(t, p).start())

    kinds = ("dn", "qu", "vu", "od", "ou")

    def z_copy(m, block, slot, to):
        st, rc = getattr(r, kinds[m] + "s"), getattr(r, kinds[m] + "r")
        return remote(st.at[block], rc.at[slot], r.z_s.at[m, to], r.z_r.at[m, slot], inst=to)

    def send_kind(m):
        loads[kinds[m]].wait()
        have, st, rc = (getattr(r, kinds[m] + e) for e in "vsr")
        if kinds[m] == "vu":
            st[...] = jnp.zeros_like(st)

        def stage(j):
            block = have[r.tabs[j]]
            if kinds[m] == "vu":
                st[j, :, 0:64] = block
            else:
                st[j] = block

        loop(0, NI, stage)
        peers(i, NI, lambda p: z_copy(m, p, i, p).start())
        rc[i] = st[i]

    send_kind(0)

    peers(t, NT, lambda p: ss_copy(p, p).wait_recv())
    total = jnp.sum(r.ssb[...], axis=0)
    gain = r.gain[...].astype(F32)
    normed = []
    for s in range(2):
        column = jnp.sum(jnp.where(eye, total[s : s + 1, :], 0.0), axis=1, keepdims=True)
        scale = lax.rsqrt(column * (1.0 / D) + NORM_EPS)
        normed.append(r.hidv[s].astype(F32) * scale * gain)
    for p in range(NT):
        r.ag[t, p * OWN : (p + 1) * OWN] = jnp.concatenate(
            [n[8 * p : 8 * p + 8] for n in normed], axis=0
        ).astype(BF16)

    def ag_ref(block, p, half):
        if half is None:
            return r.ag.at[block, pl.ds(p * 128, 128)]
        return r.ag.at[block, pl.ds(p * 128 + half * 64, 64)]

    start, steps, sent1 = mesh_gather(x, y, ag_ref, r.ag_s, r.ag_r)
    start()

    for m in range(1, 5):
        send_kind(m)

    load("wq", r.wq, r.wqv)
    r.wkv[...] = jnp.zeros_like(r.wkv)
    lane0 = pl.multiple_of(32 * lax.rem(t, 4), 32)
    load("wk", r.wk, r.wkv.at[pl.ds(lane0, 32)])
    load("wv", r.wv, r.wkv.at[pl.ds(128 + lane0, 32)])
    load("kc", r.kc, r.kext.at[:, pl.ds(0, LMAX)])
    load("vc", r.vc, r.vext.at[:, pl.ds(0, LMAX)])
    steps[0]()
    steps[1]()
    for ref in (r.qcat, r.vcat, r.oucat, r.qacc, r.kvacc, r.rs2s):
        ref[...] = jnp.zeros_like(ref)
    for step in steps[2:]:
        step()

    def wo_src(p):
        return r.wo.at[pl.ds(core * 128, 128), pl.ds(pl.multiple_of(p * SH, SH), SH)]

    def wo_copy(row, to):
        return remote(wo_src(to), r.wof.at[row, core], r.wo_s.at[to], r.wo_r.at[row], tp=to)

    peers(t, NT, lambda p: wo_copy(t, p).start())
    load("wo", wo_src(t), r.wof.at[t, core])

    for name in ("wq", "wk", "wv"):
        loads[name].wait()

    def project(b):
        cols = pl.ds(pl.multiple_of(b * SH, SH), SH)
        block = r.ag[b]
        r.qacc[...] += dot(block, r.wqv[cols, :])
        r.kvacc[...] += dot_nt(block, r.wkv[:, cols])

    loop(0, NT, project)

    def z_wait(m):
        peers(i, NI, lambda p: z_copy(m, p, p, p).wait_recv())

    def reduce_rows(own, send, recv, gathered, s1, r1, s2, r2):
        def c1(block, slot, to):
            return remote(send.at[block], recv.at[slot], s1.at[to], r1.at[slot], tp=to)

        def c2(slot, to):
            return remote(gathered.at[slot], gathered.at[slot], s2.at[to], r2.at[slot], tp=to)

        peers(t, NT, lambda p: c1(p, t, p).start())
        recv[t] = send[t]
        peers(t, NT, lambda p: c1(p, p, p).wait_recv())
        gathered[t] = jnp.sum(recv[...], axis=0).astype(BF16)
        peers(t, NT, lambda p: c2(t, p).start())
        peers(t, NT, lambda p: c2(p, p).wait_recv())

        def finish():
            peers(t, NT, lambda p: c1(p, p, p).wait_send())
            peers(t, NT, lambda p: c2(p, p).wait_send())

        return gathered[...].reshape(R2, 128).astype(F32), finish

    slot_of_row = r.rmask[...]
    z_wait(0)
    mine = r.ag[t]
    part = jnp.zeros((R2, 128), F32)
    for k in range(SLOTS):
        got = dot(mine, r.dnr[r.tabs[NI + k]])
        part = jnp.where(slot_of_row == k, got, part)
    r.rs1s[...] = part.reshape(NT, OWN, 128)
    rank, finish1 = reduce_rows(
        t, r.rs1s, r.rs1r, r.rk1, r.rs1_s, r.rs1_r, r.rk1_s, r.rk1_r
    )
    rolled = pltpu.roll(rank, 64, 1)
    for k in range(SLOTS):
        cols = slice(k * 128, (k + 1) * 128)
        r.rall[:, cols] = jnp.where(slot_of_row == k, rank, 0.0).astype(BF16)
        r.rall2[:, cols] = jnp.where(slot_of_row == k, rolled, 0.0).astype(BF16)

    z_wait(1)
    z_wait(2)
    for k in range(SLOTS):
        r.qcat[k * 128 : k * 128 + 64] = r.qur[r.tabs[NI + k]]
        r.vcat[pl.ds(lane0, 32), k * 128 : (k + 1) * 128] = r.vur[r.tabs[NI + k]]
    query = r.qacc[...] + ADAPTER_SCALING * dot(r.rall[...], r.qcat[...])
    fresh_value = r.kvacc[:, 128:] + ADAPTER_SCALING * dot_nt(r.rall2[...], r.vcat[...])
    r.qkvs[:, :, 0:256] = query.astype(BF16).reshape(NT, OWN, 256)
    r.qkvs[:, :, 256:384] = r.kvacc[:, :128].astype(BF16).reshape(NT, OWN, 128)
    r.qkvs[:, :, 384:512] = fresh_value.astype(BF16).reshape(NT, OWN, 128)

    def qkv_copy(block, slot, to):
        return remote(r.qkvs.at[block], r.qkvr.at[slot], r.qkv_s.at[to], r.qkv_r.at[slot], tp=to)

    peers(t, NT, lambda p: qkv_copy(p, t, p).start())
    r.qkvr[t] = r.qkvs[t]

    loads["wo"].wait()
    peers(t, NT, lambda p: wo_copy(p, p).wait_recv())
    sib = remote(
        r.wof.at[:, core], r.wof.at[:, core], r.sib_s.at[0], r.sib_r.at[0], inst=sibling
    )
    sib.start()

    row = lax.broadcasted_iota(jnp.int32, (OWN, HD), 0)
    lane = lax.broadcasted_iota(jnp.int32, (OWN, HD), 1)
    step_of_row = row // 8
    positions = step_of_row
    for b in range(8):
        positions = positions + jnp.where(lax.rem(row, 8) == b, r.lens[b], 0)
    freq = jnp.exp(lax.rem(lane, 64).astype(F32) * (-math.log(ROPE_BASE) / 64))
    angle = positions.astype(F32) * freq
    cos2 = jnp.cos(angle)
    sin2 = jnp.sin(angle)
    sin2 = jnp.where(lane < 64, -sin2, sin2)

    def rotate(v):
        return v * cos2 + pltpu.roll(v, 64, 1) * sin2

    peers(t, NT, lambda p: qkv_copy(p, p, p).wait_recv())
    loads["kc"].wait()
    loads["vc"].wait()
    for b in range(NT):
        for h in range(2):
            head = r.qkvr[b, :, h * HD : (h + 1) * HD].astype(F32)
            r.q2[pl.ds(2 * b + h, OWN, stride=HEADS)] = rotate(head)
    for g in range(4):
        cols = slice(g * HD, (g + 1) * HD)
        key = jnp.zeros((OWN, HD), F32)
        val = jnp.zeros((OWN, HD), F32)
        for b in range(4 * g, 4 * g + 4):
            key += r.qkvr[b, :, 256:384].astype(F32)
            val += r.qkvr[b, :, 384:512].astype(F32)
        key = rotate(key)
        for b in range(8):
            for v, ref in ((key, r.kext), (val, r.vext)):
                ref[b, LMAX:LPAD, cols] = jnp.where(
                    row == 0, v[b : b + 1], jnp.where(row == 1, v[8 + b : 9 + b], 0.0)
                ).astype(BF16)
    at_key = lax.broadcasted_iota(jnp.int32, (OWN, LPAD), 1)
    at_step = lax.broadcasted_iota(jnp.int32, (OWN, LPAD), 0) // 8
    for b in range(8):
        live = at_key < jnp.where(at_key < LMAX, r.lens[b], LMAX + 1 + at_step)
        for g in range(4):
            cols = slice(g * HD, (g + 1) * HD)
            q = jnp.concatenate(
                [
                 r.q2[(s * 8 + b) * HEADS + 8 * g : (s * 8 + b) * HEADS + 8 * g + 8]
                 for s in range(2)], axis=0
            ).astype(BF16)
            score = dot_nt(q, r.kext[b, :, cols]) * (1.0 / math.sqrt(HD))
            score = jnp.where(live, score, -jnp.inf)
            power = jnp.exp(score - jnp.max(score, axis=1, keepdims=True))
            weight = (power / jnp.sum(power, axis=1, keepdims=True)).astype(BF16)
            mix = dot(weight, r.vext[b, :, cols])
            for s in range(2):
                lo = (s * 8 + b) * HEADS + 8 * g
                r.o2[lo : lo + 8] = mix[s * 8 : s * 8 + 8]
    for h in range(HEADS):
        r.ag2[t, :, h * HD : (h + 1) * HD] = r.o2[pl.ds(h, OWN, stride=HEADS)].astype(BF16)

    def at_copy(cols_of, slot, to):
        src = r.ag2.at[t, :, pl.ds(pl.multiple_of(cols_of * 256, 256), 256)]
        return remote(src, r.attd.at[slot], r.at_s.at[to], r.at_r.at[slot], tp=to)

    peers(t, NT, lambda p: at_copy(p, t, p).start())

    def ag2_ref(block, p, half):
        if half is None:
            return r.ag2.at[block, :, pl.ds(p * 2048, 2048)]
        return r.ag2.at[block, :, pl.ds(p * 2048 + half * 1024, 1024)]

    start, steps, sent2 = mesh_gather(x, y, ag2_ref, r.ag2_s, r.ag2_r)
    start()
    r.attd[t] = r.ag2[t, :, pl.ds(pl.multiple_of(t * 256, 256), 256)]
    z_wait(3)
    steps[0]()
    steps[1]()
    peers(t, NT, lambda p: at_copy(p, p, p).wait_recv())
    heads = r.attd[...].reshape(R2, 256)
    part = jnp.zeros((R2, 64), F32)
    for k in range(SLOTS):
        got = dot_nt(heads, r.odr[r.tabs[NI + k]])
        part = jnp.where(slot_of_row[:, :64] == k, got, part)
    r.rs2s[:, :, 0:64] = part.reshape(NT, OWN, 64)
    for step in steps[2:4]:
        step()
    rank, finish2 = reduce_rows(
        t, r.rs2s, r.rs2r, r.rk2, r.rs2_s, r.rs2_r, r.rk2_s, r.rk2_r
    )
    for k in range(SLOTS):
        cols = slice(k * 128, (k + 1) * 128)
        r.rall[:, cols] = jnp.where(slot_of_row == k, rank, 0.0).astype(BF16)
    for step in steps[4:]:
        step()

    sib_in = remote(
        r.wof.at[:, 1 - core], r.wof.at[:, 1 - core], r.sib_s.at[0], r.sib_r.at[0], inst=sibling
    )
    sib_in.wait_recv()
    r.oacc[...] = jnp.zeros_like(r.oacc)

    def out_chunk(c):
        lhs = r.ag2[:, :, pl.ds(pl.multiple_of(c * 512, 512), 512)].reshape(R2, 512)
        rhs = r.wof[pl.ds(c * 2, 2)].reshape(512, SH)
        r.oacc[...] += dot(lhs, rhs)

    loop(0, 8, out_chunk)
    z_wait(4)
    for k in range(SLOTS):
        r.oucat[k * 128 : k * 128 + 64] = r.our[r.tabs[NI + k]]
    res = r.oacc[...] + ADAPTER_SCALING * dot(r.rall[...], r.oucat[...])
    for p in range(NT):
        for s in range(2):
            lo = p * OWN + s * 8
            r.oacc[s * ROWS + p * 8 : s * ROWS + p * 8 + 8] = res[lo : lo + 8]
    for s in range(2):
        r.out[s] = r.oacc[s * ROWS : (s + 1) * ROWS].astype(BF16)

    peers(t, NT, lambda p: ss_copy(p, p).wait_send())
    for m in range(5):
        peers(i, NI, lambda p, m=m: z_copy(m, p, p, p).wait_send())
    for c in sent1 + sent2:
        c.wait_send()
    peers(t, NT, lambda p: wo_copy(p, p).wait_send())
    sib.wait_send()
    peers(t, NT, lambda p: qkv_copy(p, p, p).wait_send())
    peers(t, NT, lambda p: at_copy(p, p, p).wait_send())
    finish1()
    finish2()


def local(
    hidden_in,
    norm_gain,
    query_weight,
    w_key,
    value_weight,
    w_output,
    paired_down_matrices,
    query_up_matrices,
    value_up_matrices,
    output_down_matrices,
    output_up_matrices,
    key_cache,
    value_cache,
    cache_lengths,
    row_adapter,
    old_slot,
    new_slot,
):
    i = lax.axis_index("inst")
    ids = jnp.arange(NI, dtype=jnp.int32)
    leaving = (old_slot // SLOTS == i)[None, :] & ((new_slot // SLOTS)[None, :] == ids[:, None])
    source = jnp.sum(jnp.where(leaving, (old_slot % SLOTS)[None, :], 0), axis=1)
    arriving = new_slot[None, :] == (i * SLOTS + jnp.arange(SLOTS, dtype=jnp.int32))[:, None]
    anchor = jnp.sum(jnp.where(arriving, (old_slot // SLOTS)[None, :], 0), axis=1)
    tabs = jnp.concatenate([source, anchor])
    named = row_adapter[:, None] == jnp.arange(new_slot.shape[0], dtype=jnp.int32)[None, :]
    row_slot = jnp.sum(jnp.where(named, (new_slot - i * SLOTS)[None, :], 0), axis=1)
    rmask = jnp.broadcast_to(row_slot.reshape(NT, 1, 8, 1), (NT, 2, 8, 128)).reshape(R2, 128)
    smem = pl.BlockSpec(memory_space=pltpu.SMEM)
    vmem = pl.BlockSpec(memory_space=pltpu.VMEM)
    hbm = pl.BlockSpec(memory_space=pl.ANY)
    return pl.pallas_call(
        kernel,
        out_shape=jax.ShapeDtypeStruct((2, ROWS, SH), BF16),
        in_specs=[smem, smem, vmem, vmem] + [hbm] * 12,
        out_specs=vmem,
        scratch_shapes=[pltpu.VMEM(*s) for s in SCRATCH.values()]
        + [pltpu.SemaphoreType.DMA(s) for s in SEMS.values()],
        compiler_params=pltpu.CompilerParams(
            collective_id=0, has_side_effects=True, vmem_limit_bytes=58 * 2**20
        ),
        name="decode_block",
    )(
        tabs,
        cache_lengths,
        norm_gain.reshape(1, SH),
        rmask,
        hidden_in,
        query_weight,
        w_key.T,
        value_weight.T,
        w_output,
        paired_down_matrices,
        query_up_matrices,
        jnp.swapaxes(value_up_matrices, 1, 2),
        output_down_matrices,
        output_up_matrices,
        key_cache,
        value_cache,
    )


def solution(mesh):
    placed = (
        P(None, "inst", "tp"),
        P("tp"),
        P(None, "tp"),
        P(None, "tp"),
        P(None, "tp"),
        P("tp", None),
        P("inst", "tp", None),
        P("inst", None, "tp"),
        P("inst", None, "tp"),
        P("inst", None, "tp"),
        P("inst", None, "tp"),
        P(("inst", "tp"), None, None),
        P(("inst", "tp"), None, None),
        P(("inst", "tp")),
        P("inst"),
        P(),
        P(),
    )
    return jax.shard_map(
        local, mesh=mesh, in_specs=placed, out_specs=P(None, "inst", "tp"), check_vma=False
    )
```

time: 459 us -> 140 us (0.31)
  blocking collectives: 179 us -> 0 us
  waiting for transfers between devices: 137 us -> 0 us
  Pallas kernels: 0 us -> 132 us
  starting transfers between devices: 54.6 us -> 0 us
  matrix products: 40.8 us -> 0 us
  between operations: 13.9 us -> 0.03 us
  local copies, waits for them, and re-layouts: 17.2 us -> 3.87 us
  other arithmetic: 15.4 us -> 3.74 us
    psum x2 -> x0, blocking collectives: 134 us -> none  [the longest x1 67.8 us: local(): lax.psum(select_slots(down_slots, row_choice), 'tp').astype(jnp.bfloat16)]
    pallas_call x0 -> x1, Pallas kernels: none -> 132 us  [local(): pl.pallas_call(kernel, out_shape=jax.ShapeDtypeStruct((2, ROWS, SH), BF16...]
    all_to_all x9 -> x0, waiting for transfers between devices: 75.1 us -> none  [the longest x1 26.2 us: local(): lax.all_to_all(route_slots(output_up_matrices, send_routes), 'inst', spli...]
    all_to_all x9 -> x0, starting transfers between devices: 54.5 us -> none  [the longest x2 17.2 us: local(): lax.all_to_all(jnp.concatenate([key_new, value_updated], axis=1), 'tp', s...]
    dot_general x35 -> x0, matrix products: 40.8 us -> none  [the longest x2 9.74 us: local(): lax.dot_general(w_output, attended_heads, (((0,), (1,)), ((), ())), prefe...]
    all_gather x2 -> x0, waiting for transfers between devices: 37 us -> none  [local(): lax.all_gather(current, 'tp', axis=1, tiled=True)]
    reduce_scatter x2 -> x0, waiting for transfers between devices: 23.9 us -> none  [local(): lax.psum_scatter(lax.dot_general(w_output, attended_heads, (((0,), (1,)),...]
    all_gather x1 -> x0, blocking collectives: 23.3 us -> none  [local(): lax.all_gather(norm_gain.reshape(1, -1), 'tp', axis=1, tiled=True)]
  transfers between devices with their start and end apart: 13 -> 0, of which waited for: 9 -> 0; matrix products, arithmetic and copies ran while one was open for 9% -> 0% of each run, Pallas kernels for 0% -> 0%
where the time goes in v1:
time: 140 us
  Pallas kernels  132 us (94%)
  local copies, waits for them, and re-layouts  3.87 us (3%)
  other arithmetic  3.74 us (3%)
    pallas_call x1, Pallas kernels, local(): pl.pallas_call(kernel, out_shape=jax.ShapeDtypeStruct((2, ROWS, SH), BF16...  132 us

profile of v1, /device:TPU:2, one launch (start us, length us, event | category | flops | bytes accessed | tf_op | source)
XLA Modules:
  0.0 139.9 jit_solution(6762964586765089298)
XLA Ops:
  0.0 0.7 broadcast_compare_fusion
  0.7 0.8 select_reduce_fusion.2
  1.5 0.7 broadcast_subtract_fusion
  2.2 0.8 select_reduce_fusion
  3.0 0.1 select_reduce_fusion.1
  3.1 0.6 pad_add_fusion.args_0_
  3.8 1.3 reshape.18.args_2_
  5.0 0.1 broadcast_in_dim.63
  5.1 0.1 broadcast_in_dim.65
  5.2 0.8 broadcast_in_dim.66.args_3_
  6.0 132.3 %decode_block.1 = bf16[2,128,512]{2,1,0:T(8,128)(2,1)} custom-call(s32[24]{0:T(128)} %pad_add_fusion.args_0_, s32[8]{0:T(128)} %args_1_.4, bf16[1,512]{1,0:T(2,128)(2,1)} %reshape.18.args_2_, s32[256,128]{1,0:T(8,128)} %broadcast_in_dim.66.args_3_, bf16[2,128,512]{2,1,0:T(8,128)(2,1)} %args_4_.4, bf16[8192,256]{1,0:T(8,128)(2,1)} %args_5_.4, ...), custom_call_target="tpu_custom_call" | custom-call | tf_op jit(solution)/shard_map/decode_block/pallas_call | solution.py:562
  138.2 1.7 %copy.19 = bf16[2,128,512]{2,1,0:T(8,128)(2,1)} copy(bf16[2,128,512]{2,1,0:T(8,128)(2,1)} %decode_block.1) | data formatting | bytes 524288
  (2 shorter events, 0.0 us)

commit v2 on v1

--- a/solution.py
+++ b/solution.py
@@ -28,9 +28,20 @@
 NORM_EPS = 1e-05
 ROPE_BASE = 500000.0
 
+WO_ORDER = (
+    (1, 0), (0, 3), (3, 0), (0, 1), (1, 1), (3, 3), (1, 3), (3, 1),
+    (2, 0), (0, 2), (2, 1), (1, 2), (2, 3), (3, 2), (2, 2),
+)
+
 SCRATCH = dict(
-    hidv=((2, ROWS, SH), BF16),
-    ag=((NT, R2, SH), BF16),
+    tabv=((8, 128), jnp.int32),
+    rmask=((R2, 128), F32),
+    ag=((NT, 2, ROWS, SH), BF16),
+    nrm=((R2, SH), BF16),
+    mine=((R2, SH), BF16),
+    gains=((NT, 1, SH), F32),
+    sc=((8 * 64, LPAD), F32),
+    wt=((8 * 64, LPAD), BF16),
     wqv=((D, 256), BF16),
     wkv=((256, D), BF16),
     wof=((NT, 2, 128, SH), BF16),
@@ -86,7 +97,7 @@
     rs2_s=(NT,), rs2_r=(NT,), rk2_s=(NT,), rk2_r=(NT,),
 )
 INPUTS = (
-    "tabs", "lens", "gain", "rmask", "hid", "wq", "wk", "wv", "wo",
+    "lens", "gain", "adapter", "old", "new", "hid", "wq", "wk", "wv", "wo",
     "dn", "qu", "vu", "od", "ou", "kc", "vc",
 )
 
@@ -203,7 +214,7 @@
 
 
 def kernel(*args):
-    names = list(INPUTS) + ["out"] + list(SCRATCH) + list(SEMS)
+    names = list(INPUTS) + ["out", "tabs"] + list(SCRATCH) + list(SEMS)
     r = Refs()
     for name, ref in zip(names, args, strict=True):
         setattr(r, name, ref)
@@ -220,7 +231,7 @@
         c.start()
         loads[name] = c
 
-    load("hid", r.hid, r.hidv)
+    load("hid", r.hid, r.ag.at[t])
     for m in ("dn", "qu", "vu", "od", "ou"):
         load(m, getattr(r, m), getattr(r, m + "v"))
 
@@ -232,16 +243,41 @@
     peers(t, NT, lambda p: hello("tp", p))
     peers(i, NI, lambda p: hello("inst", p))
 
-    eye = lax.broadcasted_iota(jnp.int32, (128, 128), 0) == lax.broadcasted_iota(
-        jnp.int32, (128, 128), 1
-    )
+    sub = lax.broadcasted_iota(jnp.int32, (128, 128), 0)
+    lan = lax.broadcasted_iota(jnp.int32, (128, 128), 1)
+    eye = sub == lan
+
+    def to_column(v):
+        return jnp.sum(jnp.where(eye, v, 0.0), axis=1, keepdims=True)
+
+    def to_row(v):
+        return jnp.sum(jnp.where(eye, v, 0.0), axis=0, keepdims=True)
+
+    old, new = r.old[...], r.new[...]
+    goes = ((old >> 3) == i) & ((new >> 3) == sub) & (sub < NI)
+    comes = (new == i * SLOTS + sub - NI) & (sub >= NI) & (sub < NI + SLOTS)
+    table = jnp.where(goes, old & 7, 0) + jnp.where(comes, old >> 3, 0)
+    table = jnp.sum(table, axis=1, keepdims=True)
+    table = jnp.sum(jnp.where(eye, table, 0), axis=0, keepdims=True)
+    r.tabv[...] = jnp.broadcast_to(table, (8, 128))
+    load("tabs", r.tabv, r.tabs)
+    named = to_column(r.adapter[...].astype(F32)) == lan.astype(F32)
+    slot_column = jnp.sum(jnp.where(named, new.astype(F32), 0.0), axis=1, keepdims=True)
+    slot_column = jnp.broadcast_to(slot_column - (i * SLOTS).astype(F32), (128, 128))
+    for p in range(NT):
+        for s in range(2):
+            r.rmask[p * OWN + s * 8 : p * OWN + s * 8 + 8] = slot_column[8 * p : 8 * p + 8]
+
+    def entry(n, top):
+        return jnp.clip(r.tabs[0, n], 0, top - 1)
+
     loads["hid"].wait()
     parts = []
     for s in range(2):
-        h = r.hidv[s].astype(F32)
-        column = jnp.sum(h * h, axis=1, keepdims=True)
-        parts.append(jnp.sum(jnp.where(eye, column, 0.0), axis=0, keepdims=True))
-    r.ssb[t] = jnp.concatenate(parts + [jnp.zeros((6, 128), F32)], axis=0)
+        h = r.ag[t, s].astype(F32)
+        parts.append(to_row(jnp.sum(h * h, axis=1, keepdims=True)))
+    gain = r.gain[...].astype(F32)
+    r.ssb[t] = jnp.concatenate(parts + [gain, jnp.zeros((2, 128), F32)], axis=0)
 
     pl.semaphore_wait(bar, NT + NI - 2)
 
@@ -251,6 +287,15 @@
         )
 
     peers(t, NT, lambda p: ss_copy(t, p).start())
+
+    def ag_ref(block, p, half):
+        if half is None:
+            return r.ag.at[block, p]
+        return r.ag.at[block, p, pl.ds(half * 64, 64)]
+
+    start, steps, sent1 = mesh_gather(x, y, ag_ref, r.ag_s, r.ag_r)
+    start()
+    loads["tabs"].wait()
 
     kinds = ("dn", "qu", "vu", "od", "ou")
 
@@ -265,7 +310,7 @@
             st[...] = jnp.zeros_like(st)
 
         def stage(j):
-            block = have[r.tabs[j]]
+            block = have[entry(j, SLOTS)]
             if kinds[m] == "vu":
                 st[j, :, 0:64] = block
             else:
@@ -276,27 +321,6 @@
         rc[i] = st[i]
 
     send_kind(0)
-
-    peers(t, NT, lambda p: ss_copy(p, p).wait_recv())
-    total = jnp.sum(r.ssb[...], axis=0)
-    gain = r.gain[...].astype(F32)
-    normed = []
-    for s in range(2):
-        column = jnp.sum(jnp.where(eye, total[s : s + 1, :], 0.0), axis=1, keepdims=True)
-        scale = lax.rsqrt(column * (1.0 / D) + NORM_EPS)
-        normed.append(r.hidv[s].astype(F32) * scale * gain)
-    for p in range(NT):
-        r.ag[t, p * OWN : (p + 1) * OWN] = jnp.concatenate(
-            [n[8 * p : 8 * p + 8] for n in normed], axis=0
-        ).astype(BF16)
-
-    def ag_ref(block, p, half):
-        if half is None:
-            return r.ag.at[block, pl.ds(p * 128, 128)]
-        return r.ag.at[block, pl.ds(p * 128 + half * 64, 64)]
-
-    start, steps, sent1 = mesh_gather(x, y, ag_ref, r.ag_s, r.ag_r)
-    start()
 
     for m in range(1, 5):
         send_kind(m)
@@ -312,8 +336,6 @@
     steps[1]()
     for ref in (r.qcat, r.vcat, r.oucat, r.qacc, r.kvacc, r.rs2s):
         ref[...] = jnp.zeros_like(ref)
-    for step in steps[2:]:
-        step()
 
     def wo_src(p):
         return r.wo.at[pl.ds(core * 128, 128), pl.ds(pl.multiple_of(p * SH, SH), SH)]
@@ -321,19 +343,48 @@
     def wo_copy(row, to):
         return remote(wo_src(to), r.wof.at[row, core], r.wo_s.at[to], r.wo_r.at[row], tp=to)
 
-    peers(t, NT, lambda p: wo_copy(t, p).start())
     load("wo", wo_src(t), r.wof.at[t, core])
-
+    for n, step in enumerate(steps[2:]):
+        step()
+        for dx, dy in WO_ORDER[3 * n : 3 * n + 3]:
+            ox, oy = dx + core * (dy - dx), dy + core * (dx - dy)
+            p = lax.rem(x + ox, SIDE) * SIDE + lax.rem(y + oy, SIDE)
+            wo_copy(t, p).start()
+
+    peers(t, NT, lambda p: ss_copy(p, p).wait_recv())
+    total = jnp.sum(r.ssb[...], axis=0)
+    scale = [
+        lax.rsqrt(to_column(total[s : s + 1, :]) * (1.0 / D) + NORM_EPS) for s in range(2)
+    ]
+    for b in range(NT):
+        r.gains[b] = jnp.concatenate([r.ssb[b, 2 + q : 3 + q, :] for q in range(4)], axis=1)
+
+    def normalise(b, dst):
+        gain = r.gains[b]
+        n0, n1 = (r.ag[b, s].astype(F32) * scale[s] * gain for s in range(2))
+        for p in range(NT):
+            rows = slice(8 * p, 8 * p + 8)
+            dst[p * OWN : (p + 1) * OWN] = jnp.concatenate([n0[rows], n1[rows]], axis=0).astype(BF16)
+
+    normalise(t, r.mine)
     for name in ("wq", "wk", "wv"):
         loads[name].wait()
 
     def project(b):
         cols = pl.ds(pl.multiple_of(b * SH, SH), SH)
-        block = r.ag[b]
+        normalise(b, r.nrm)
+        block = r.nrm[...]
         r.qacc[...] += dot(block, r.wqv[cols, :])
         r.kvacc[...] += dot_nt(block, r.wkv[:, cols])
 
     loop(0, NT, project)
+
+    loads["wo"].wait()
+    peers(t, NT, lambda p: wo_copy(p, p).wait_recv())
+    sib = remote(
+        r.wof.at[:, core], r.wof.at[:, core], r.sib_s.at[0], r.sib_r.at[0], inst=sibling
+    )
+    sib.start()
 
     def z_wait(m):
         peers(i, NI, lambda p: z_copy(m, p, p, p).wait_recv())
@@ -360,11 +411,11 @@
 
     slot_of_row = r.rmask[...]
     z_wait(0)
-    mine = r.ag[t]
+    mine = r.mine[...]
     part = jnp.zeros((R2, 128), F32)
     for k in range(SLOTS):
-        got = dot(mine, r.dnr[r.tabs[NI + k]])
-        part = jnp.where(slot_of_row == k, got, part)
+        got = dot(mine, r.dnr[entry(NI + k, NI)])
+        part = jnp.where(slot_of_row == float(k), got, part)
     r.rs1s[...] = part.reshape(NT, OWN, 128)
     rank, finish1 = reduce_rows(
         t, r.rs1s, r.rs1r, r.rk1, r.rs1_s, r.rs1_r, r.rk1_s, r.rk1_r
@@ -372,14 +423,14 @@
     rolled = pltpu.roll(rank, 64, 1)
     for k in range(SLOTS):
         cols = slice(k * 128, (k + 1) * 128)
-        r.rall[:, cols] = jnp.where(slot_of_row == k, rank, 0.0).astype(BF16)
-        r.rall2[:, cols] = jnp.where(slot_of_row == k, rolled, 0.0).astype(BF16)
+        r.rall[:, cols] = jnp.where(slot_of_row == float(k), rank, 0.0).astype(BF16)
+        r.rall2[:, cols] = jnp.where(slot_of_row == float(k), rolled, 0.0).astype(BF16)
 
     z_wait(1)
     z_wait(2)
     for k in range(SLOTS):
-        r.qcat[k * 128 : k * 128 + 64] = r.qur[r.tabs[NI + k]]
-        r.vcat[pl.ds(lane0, 32), k * 128 : (k + 1) * 128] = r.vur[r.tabs[NI + k]]
+        r.qcat[k * 128 : k * 128 + 64] = r.qur[entry(NI + k, NI)]
+        r.vcat[pl.ds(lane0, 32), k * 128 : (k + 1) * 128] = r.vur[entry(NI + k, NI)]
     query = r.qacc[...] + ADAPTER_SCALING * dot(r.rall[...], r.qcat[...])
     fresh_value = r.kvacc[:, 128:] + ADAPTER_SCALING * dot_nt(r.rall2[...], r.vcat[...])
     r.qkvs[:, :, 0:256] = query.astype(BF16).reshape(NT, OWN, 256)
@@ -391,13 +442,6 @@
 
     peers(t, NT, lambda p: qkv_copy(p, t, p).start())
     r.qkvr[t] = r.qkvs[t]
-
-    loads["wo"].wait()
-    peers(t, NT, lambda p: wo_copy(p, p).wait_recv())
-    sib = remote(
-        r.wof.at[:, core], r.wof.at[:, core], r.sib_s.at[0], r.sib_r.at[0], inst=sibling
-    )
-    sib.start()
 
     row = lax.broadcasted_iota(jnp.int32, (OWN, HD), 0)
     lane = lax.broadcasted_iota(jnp.int32, (OWN, HD), 1)
@@ -434,22 +478,24 @@
                 ref[b, LMAX:LPAD, cols] = jnp.where(
                     row == 0, v[b : b + 1], jnp.where(row == 1, v[8 + b : 9 + b], 0.0)
                 ).astype(BF16)
-    at_key = lax.broadcasted_iota(jnp.int32, (OWN, LPAD), 1)
-    at_step = lax.broadcasted_iota(jnp.int32, (OWN, LPAD), 0) // 8
     for b in range(8):
+        for g in range(4):
+            lo = [(s * 8 + b) * HEADS + 8 * g for s in range(2)]
+            q = jnp.concatenate([r.q2[o : o + 8] for o in lo], axis=0).astype(BF16)
+            score = dot_nt(q, r.kext[b, :, g * HD : (g + 1) * HD])
+            r.sc[(b * 4 + g) * OWN : (b * 4 + g + 1) * OWN] = score * (1.0 / math.sqrt(HD))
+    at_key = lax.broadcasted_iota(jnp.int32, (64, LPAD), 1)
+    at_step = lax.rem(lax.broadcasted_iota(jnp.int32, (64, LPAD), 0) // 8, 2)
+    for b in range(8):
+        rows = slice(b * 64, (b + 1) * 64)
         live = at_key < jnp.where(at_key < LMAX, r.lens[b], LMAX + 1 + at_step)
+        score = jnp.where(live, r.sc[rows], -jnp.inf)
+        power = jnp.exp(score - jnp.max(score, axis=1, keepdims=True))
+        r.wt[rows] = (power / jnp.sum(power, axis=1, keepdims=True)).astype(BF16)
+    for b in range(8):
         for g in range(4):
-            cols = slice(g * HD, (g + 1) * HD)
-            q = jnp.concatenate(
-                [
-                 r.q2[(s * 8 + b) * HEADS + 8 * g : (s * 8 + b) * HEADS + 8 * g + 8]
-                 for s in range(2)], axis=0
-            ).astype(BF16)
-            score = dot_nt(q, r.kext[b, :, cols]) * (1.0 / math.sqrt(HD))
-            score = jnp.where(live, score, -jnp.inf)
-            power = jnp.exp(score - jnp.max(score, axis=1, keepdims=True))
-            weight = (power / jnp.sum(power, axis=1, keepdims=True)).astype(BF16)
-            mix = dot(weight, r.vext[b, :, cols])
+            weight = r.wt[(b * 4 + g) * OWN : (b * 4 + g + 1) * OWN]
+            mix = dot(weight, r.vext[b, :, g * HD : (g + 1) * HD])
             for s in range(2):
                 lo = (s * 8 + b) * HEADS + 8 * g
                 r.o2[lo : lo + 8] = mix[s * 8 : s * 8 + 8]
@@ -477,8 +523,8 @@
     heads = r.attd[...].reshape(R2, 256)
     part = jnp.zeros((R2, 64), F32)
     for k in range(SLOTS):
-        got = dot_nt(heads, r.odr[r.tabs[NI + k]])
-        part = jnp.where(slot_of_row[:, :64] == k, got, part)
+        got = dot_nt(heads, r.odr[entry(NI + k, NI)])
+        part = jnp.where(slot_of_row[:, :64] == float(k), got, part)
     r.rs2s[:, :, 0:64] = part.reshape(NT, OWN, 64)
     for step in steps[2:4]:
         step()
@@ -487,7 +533,7 @@
     )
     for k in range(SLOTS):
         cols = slice(k * 128, (k + 1) * 128)
-        r.rall[:, cols] = jnp.where(slot_of_row == k, rank, 0.0).astype(BF16)
+        r.rall[:, cols] = jnp.where(slot_of_row == float(k), rank, 0.0).astype(BF16)
     for step in steps[4:]:
         step()
 
@@ -505,7 +551,7 @@
     loop(0, 8, out_chunk)
     z_wait(4)
     for k in range(SLOTS):
-        r.oucat[k * 128 : k * 128 + 64] = r.our[r.tabs[NI + k]]
+        r.oucat[k * 128 : k * 128 + 64] = r.our[entry(NI + k, NI)]
     res = r.oacc[...] + ADAPTER_SCALING * dot(r.rall[...], r.oucat[...])
     for p in range(NT):
         for s in range(2):
@@ -546,35 +592,27 @@
     old_slot,
     new_slot,
 ):
-    i = lax.axis_index("inst")
-    ids = jnp.arange(NI, dtype=jnp.int32)
-    leaving = (old_slot // SLOTS == i)[None, :] & ((new_slot // SLOTS)[None, :] == ids[:, None])
-    source = jnp.sum(jnp.where(leaving, (old_slot % SLOTS)[None, :], 0), axis=1)
-    arriving = new_slot[None, :] == (i * SLOTS + jnp.arange(SLOTS, dtype=jnp.int32))[:, None]
-    anchor = jnp.sum(jnp.where(arriving, (old_slot // SLOTS)[None, :], 0), axis=1)
-    tabs = jnp.concatenate([source, anchor])
-    named = row_adapter[:, None] == jnp.arange(new_slot.shape[0], dtype=jnp.int32)[None, :]
-    row_slot = jnp.sum(jnp.where(named, (new_slot - i * SLOTS)[None, :], 0), axis=1)
-    rmask = jnp.broadcast_to(row_slot.reshape(NT, 1, 8, 1), (NT, 2, 8, 128)).reshape(R2, 128)
     smem = pl.BlockSpec(memory_space=pltpu.SMEM)
     vmem = pl.BlockSpec(memory_space=pltpu.VMEM)
     hbm = pl.BlockSpec(memory_space=pl.ANY)
     return pl.pallas_call(
         kernel,
         out_shape=jax.ShapeDtypeStruct((2, ROWS, SH), BF16),
-        in_specs=[smem, smem, vmem, vmem] + [hbm] * 12,
+        in_specs=[smem] + [vmem] * 4 + [hbm] * 12,
         out_specs=vmem,
-        scratch_shapes=[pltpu.VMEM(*s) for s in SCRATCH.values()]
+        scratch_shapes=[pltpu.SMEM((8, 128), jnp.int32)]
+        + [pltpu.VMEM(*s) for s in SCRATCH.values()]
         + [pltpu.SemaphoreType.DMA(s) for s in SEMS.values()],
         compiler_params=pltpu.CompilerParams(
             collective_id=0, has_side_effects=True, vmem_limit_bytes=58 * 2**20
         ),
         name="decode_block",
     )(
-        tabs,
         cache_lengths,
-        norm_gain.reshape(1, SH),
-        rmask,
+        norm_gain.reshape(4, 128),
+        row_adapter.reshape(1, ROWS),
+        old_slot.reshape(1, -1),
+        new_slot.reshape(1, -1),
         hidden_in,
         query_weight,
         w_key.T,

time: 140 us -> 123 us (0.88)
  Pallas kernels: 132 us -> 121 us
  other arithmetic: 3.74 us -> 0 us
  local copies, waits for them, and re-layouts: 3.87 us -> 1.67 us
    pallas_call x1, Pallas kernels: 132 us -> 121 us  [local(): pl.pallas_call(kernel, out_shape=jax.ShapeDtypeStruct((2, ROWS, SH), BF16...]
    reduce_sum x3 -> x0, other arithmetic: 1.77 us -> none  [the longest x1 0.83 us: local(): jnp.sum(jnp.where(arriving, (old_slot // SLOTS)[None, :], 0), axis=1)]
where the time goes in v2:
time: 123 us
  Pallas kernels  121 us (98%)
  local copies, waits for them, and re-layouts  1.67 us (1%)
    pallas_call x1, Pallas kernels, local(): pl.pallas_call(kernel, out_shape=jax.ShapeDtypeStruct((2, ROWS, SH), BF16...  121 us

profile of v2, /device:TPU:2, one launch (start us, length us, event | category | flops | bytes accessed | tf_op | source)
XLA Modules:
  0.0 122.8 jit_solution(3574858811343108879)
XLA Ops:
  0.0 121.1 %decode_block.1 = bf16[2,128,512]{2,1,0:T(8,128)(2,1)} custom-call(s32[8]{0:T(128)} %args_0_.4, bf16[4,128]{1,0:T(4,128)(2,1)} %bitcast.10, s32[1,128]{1,0:T(1,128)} %bitcast.11, s32[1,128]{1,0:T(1,128)} %bitcast.12, s32[1,128]{1,0:T(1,128)} %bitcast.13, bf16[2,128,512]{2,1,0:T(8,128)(2,1)} %args_5_.4, bf16[8192,256]{1,0:T(8,128)(2,1)} %args_6_.4, ...), custom_call_target="tpu_custom_call" | custom-call | tf_op jit(solution)/shard_map/decode_block/pallas_call | solution.py:598
  121.1 1.7 %copy.19 = bf16[2,128,512]{2,1,0:T(8,128)(2,1)} copy(bf16[2,128,512]{2,1,0:T(8,128)(2,1)} %decode_block.1) | data formatting | bytes 524288

commit v3 on v2

--- a/solution.py
+++ b/solution.py
@@ -13,6 +13,7 @@
 
 NT = 16
 NI = 16
+NZ = 8
 SIDE = 4
 D = 8192
 SH = 512
@@ -38,24 +39,28 @@
     rmask=((R2, 128), F32),
     ag=((NT, 2, ROWS, SH), BF16),
     nrm=((R2, SH), BF16),
-    mine=((R2, SH), BF16),
     gains=((NT, 1, SH), F32),
     sc=((8 * 64, LPAD), F32),
     wt=((8 * 64, LPAD), BF16),
     wqv=((D, 256), BF16),
     wkv=((256, D), BF16),
     wof=((NT, 2, 128, SH), BF16),
-    dnv=((SLOTS, SH, 128), BF16),
+    dn2=((SLOTS, SH, 256), BF16),
+    zb=((NZ, 2, ROWS, SH), BF16),
+    zsb=((NZ, 8, 128), F32),
+    zmask=((R2, 128), F32),
+    ps=((NT, NZ, OWN, 128), BF16),
+    pr=((NT, NZ, OWN, 128), BF16),
+    rrs=((NZ, OWN, 128), BF16),
+    rr=((NZ, OWN, 128), BF16),
     quv=((SLOTS, 64, 256), BF16),
     vuv=((SLOTS, 32, 64), BF16),
     odv=((SLOTS, 64, 256), BF16),
     ouv=((SLOTS, 64, SH), BF16),
-    dns=((NI, SH, 128), BF16),
     qus=((NI, 64, 256), BF16),
     vus=((NI, 32, 128), BF16),
     ods=((NI, 64, 256), BF16),
     ous=((NI, 64, SH), BF16),
-    dnr=((NI, SH, 128), BF16),
     qur=((NI, 64, 256), BF16),
     vur=((NI, 32, 128), BF16),
     odr=((NI, 64, 256), BF16),
@@ -68,8 +73,6 @@
     kext=((8, LPAD, 512), BF16),
     vext=((8, LPAD, 512), BF16),
     ssb=((NT, 8, 128), F32),
-    rs1s=((NT, OWN, 128), F32),
-    rs1r=((NT, OWN, 128), F32),
     rk1=((NT, OWN, 128), BF16),
     rs2s=((NT, OWN, 128), F32),
     rs2r=((NT, OWN, 128), F32),
@@ -88,9 +91,11 @@
     ld=(16,),
     ss_s=(NT,), ss_r=(NT,),
     ag_s=(2, 20), ag_r=(2, NT, 2),
-    z_s=(5, NI), z_r=(5, NI),
+    z_s=(4, NI), z_r=(4, NI),
+    zg_s=(14,), zg_r=(NZ, 2), zs_s=(NZ,), zs_r=(NZ,), dn_s=(1,), dn_r=(1,),
+    pr_s=(NT,), pr_r=(NT,), rr_s=(NZ,), rr_r=(NZ,),
     wo_s=(NT,), wo_r=(NT,), sib_s=(1,), sib_r=(1,),
-    rs1_s=(NT,), rs1_r=(NT,), rk1_s=(NT,), rk1_r=(NT,),
+    rk1_s=(NT,), rk1_r=(NT,),
     qkv_s=(NT,), qkv_r=(NT,),
     ag2_s=(2, 20), ag2_r=(2, NT, 2),
     at_s=(NT,), at_r=(NT,),
@@ -222,6 +227,7 @@
     t = lax.axis_index("tp")
     x, y = t // SIDE, lax.rem(t, SIDE)
     core = lax.rem(i, 2)
+    zc = i // 2
     sibling = i + 1 - 2 * core
 
     loads = {}
@@ -232,7 +238,10 @@
         loads[name] = c
 
     load("hid", r.hid, r.ag.at[t])
-    for m in ("dn", "qu", "vu", "od", "ou"):
+    half0 = pl.multiple_of(core * 128, 128)
+    half1 = pl.multiple_of(128 - core * 128, 128)
+    load("dn", r.dn, r.dn2.at[:, :, pl.ds(half0, 128)])
+    for m in ("qu", "vu", "od", "ou"):
         load(m, getattr(r, m), getattr(r, m + "v"))
 
     bar = pltpu.get_barrier_semaphore()
@@ -243,6 +252,55 @@
     peers(t, NT, lambda p: hello("tp", p))
     peers(i, NI, lambda p: hello("inst", p))
 
+    loads["hid"].wait()
+    pl.semaphore_wait(bar, NT + NI - 2)
+
+    def ag_ref(block, p, half):
+        if half is None:
+            return r.ag.at[block, p]
+        return r.ag.at[block, p, pl.ds(half * 64, 64)]
+
+    start, steps, sent1 = mesh_gather(x, y, ag_ref, r.ag_s, r.ag_r)
+    start()
+
+    def chip(d):
+        return lax.rem(zc + d + NZ, NZ)
+
+    def zg_copy(d, half, to, idx):
+        block = chip(d)
+        src, dst = (r.ag.at[t] if d == 0 else r.zb.at[block]), r.zb.at[block]
+        if half is not None:
+            src, dst = src.at[half], dst.at[half]
+        return remote(
+            src, dst, r.zg_s.at[idx], r.zg_r.at[block, half or 0], inst=chip(to) * 2 + core
+        )
+
+    sent_z = []
+
+    def zg_send(*what):
+        c = zg_copy(*what, len(sent_z))
+        c.start()
+        sent_z.append(c)
+
+    def zg_wait(d, half=None):
+        zg_copy(d, half, 1, 0).wait_recv()
+
+    def zg_pass(d, order):
+        for n in order:
+            for side in (-1, 1):
+                half = n if side < 0 else 1 - n
+                zg_wait(side * d, half)
+                if d < 3 or n == 0:
+                    zg_send(side * d, half, -side)
+
+    for n in range(2):
+        zg_send(0, n, 1)
+        zg_send(0, 1 - n, -1)
+    dn_out = remote(
+        r.dn, r.dn2.at[:, :, pl.ds(half0, 128)], r.dn_s.at[0], r.dn_r.at[0], inst=sibling
+    )
+    dn_out.start()
+    r.zb[zc] = r.ag[t]
     sub = lax.broadcasted_iota(jnp.int32, (128, 128), 0)
     lan = lax.broadcasted_iota(jnp.int32, (128, 128), 1)
     eye = sub == lan
@@ -252,6 +310,21 @@
 
     def to_row(v):
         return jnp.sum(jnp.where(eye, v, 0.0), axis=0, keepdims=True)
+
+    parts = []
+    for s in range(2):
+        h = r.ag[t, s].astype(F32)
+        parts.append(to_row(jnp.sum(h * h, axis=1, keepdims=True)))
+    gain = r.gain[...].astype(F32)
+    r.ssb[t] = jnp.concatenate(parts + [gain, jnp.zeros((2, 128), F32)], axis=0)
+
+    def ss_copy(src_block, to):
+        return remote(
+            r.ssb.at[src_block], r.ssb.at[src_block], r.ss_s.at[to], r.ss_r.at[src_block], tp=to
+        )
+
+    peers(t, NT, lambda p: ss_copy(t, p).start())
+
 
     old, new = r.old[...], r.new[...]
     goes = ((old >> 3) == i) & ((new >> 3) == sub) & (sub < NI)
@@ -263,6 +336,9 @@
     load("tabs", r.tabv, r.tabs)
     named = to_column(r.adapter[...].astype(F32)) == lan.astype(F32)
     slot_column = jnp.sum(jnp.where(named, new.astype(F32), 0.0), axis=1, keepdims=True)
+    old_row = to_row(
+        jnp.sum(jnp.where(named, old.astype(F32), 0.0), axis=1, keepdims=True)
+    )
     slot_column = jnp.broadcast_to(slot_column - (i * SLOTS).astype(F32), (128, 128))
     for p in range(NT):
         for s in range(2):
@@ -271,39 +347,17 @@
     def entry(n, top):
         return jnp.clip(r.tabs[0, n], 0, top - 1)
 
-    loads["hid"].wait()
-    parts = []
-    for s in range(2):
-        h = r.ag[t, s].astype(F32)
-        parts.append(to_row(jnp.sum(h * h, axis=1, keepdims=True)))
-    gain = r.gain[...].astype(F32)
-    r.ssb[t] = jnp.concatenate(parts + [gain, jnp.zeros((2, 128), F32)], axis=0)
-
-    pl.semaphore_wait(bar, NT + NI - 2)
-
-    def ss_copy(src_block, to):
-        return remote(
-            r.ssb.at[src_block], r.ssb.at[src_block], r.ss_s.at[to], r.ss_r.at[src_block], tp=to
-        )
-
-    peers(t, NT, lambda p: ss_copy(t, p).start())
-
-    def ag_ref(block, p, half):
-        if half is None:
-            return r.ag.at[block, p]
-        return r.ag.at[block, p, pl.ds(half * 64, 64)]
-
-    start, steps, sent1 = mesh_gather(x, y, ag_ref, r.ag_s, r.ag_r)
-    start()
+    steps[0]()
+    zg_pass(1, (0,))
     loads["tabs"].wait()
 
-    kinds = ("dn", "qu", "vu", "od", "ou")
+    kinds = ("qu", "vu", "od", "ou")
 
     def z_copy(m, block, slot, to):
         st, rc = getattr(r, kinds[m] + "s"), getattr(r, kinds[m] + "r")
         return remote(st.at[block], rc.at[slot], r.z_s.at[m, to], r.z_r.at[m, slot], inst=to)
 
-    def send_kind(m):
+    def stage_kind(m):
         loads[kinds[m]].wait()
         have, st, rc = (getattr(r, kinds[m] + e) for e in "vsr")
         if kinds[m] == "vu":
@@ -317,13 +371,63 @@
                 st[j] = block
 
         loop(0, NI, stage)
+        rc[i] = st[i]
+
+    def send_kind(m):
         peers(i, NI, lambda p: z_copy(m, p, i, p).start())
-        rc[i] = st[i]
-
-    send_kind(0)
-
-    for m in range(1, 5):
-        send_kind(m)
+
+    def z_wait(m):
+        peers(i, NI, lambda p: z_copy(m, p, p, p).wait_recv())
+
+    for m in range(4):
+        stage_kind(m)
+
+    peers(t, NT, lambda p: ss_copy(p, p).wait_recv())
+    total = jnp.sum(r.ssb[...], axis=0)
+    r.zsb[zc] = jnp.concatenate([total[0:2], old_row, jnp.zeros((5, 128), F32)], axis=0)
+
+    def zs_copy(block, to):
+        return remote(
+            r.zsb.at[block], r.zsb.at[block], r.zs_s.at[to], r.zs_r.at[block], inst=to * 2 + core
+        )
+
+    peers(zc, NZ, lambda p: zs_copy(zc, p).start())
+    steps[1]()
+
+    def scales(sums):
+        return [
+            lax.rsqrt(to_column(sums[s : s + 1, :]) * (1.0 / D) + NORM_EPS) for s in range(2)
+        ]
+
+    def normalise(src, scale, gain):
+        n0, n1 = (src[s].astype(F32) * scale[s] * gain for s in range(2))
+        for p in range(NT):
+            rows = slice(8 * p, 8 * p + 8)
+            r.nrm[p * OWN : (p + 1) * OWN] = jnp.concatenate(
+                [n0[rows], n1[rows]], axis=0
+            ).astype(BF16)
+
+    for b in range(NT):
+        r.gains[b] = jnp.concatenate([r.ssb[b, 2 + q : 3 + q, :] for q in range(4)], axis=1)
+    own_gain = r.gains[t]
+
+    def partial(block):
+        sums = r.zsb[block]
+        normalise(r.zb.at[block], scales(sums), own_gain)
+        slots = to_column(sums[2:3, :]) - (zc * 2 * SLOTS).astype(F32)
+        slots = jnp.broadcast_to(slots, (128, 128))
+        for p in range(NT):
+            for s in range(2):
+                lo = p * OWN + s * 8
+                r.zmask[lo : lo + 8] = slots[8 * p : 8 * p + 8]
+        mask = r.zmask[...]
+        rows = r.nrm[...]
+        part = jnp.zeros((R2, 128), F32)
+        for k in range(SLOTS):
+            got = dot(rows, r.dn2[k])
+            part = jnp.where(mask == float(k), got[:, :128], part)
+            part = jnp.where(mask == float(SLOTS + k), got[:, 128:], part)
+        r.ps[:, block] = part.astype(BF16).reshape(NT, OWN, 128)
 
     load("wq", r.wq, r.wqv)
     r.wkv[...] = jnp.zeros_like(r.wkv)
@@ -332,105 +436,110 @@
     load("wv", r.wv, r.wkv.at[pl.ds(128 + lane0, 32)])
     load("kc", r.kc, r.kext.at[:, pl.ds(0, LMAX)])
     load("vc", r.vc, r.vext.at[:, pl.ds(0, LMAX)])
-    steps[0]()
-    steps[1]()
+
+    zg_pass(1, (1,))
+    loads["dn"].wait()
+    remote(
+        r.dn, r.dn2.at[:, :, pl.ds(half1, 128)], r.dn_s.at[0], r.dn_r.at[0], inst=sibling
+    ).wait_recv()
+    steps[2]()
+    partial(zc)
+    zg_pass(2, (0,))
+    steps[3]()
+    peers(zc, NZ, lambda p: zs_copy(p, p).wait_recv())
+    partial(chip(1))
+    zg_pass(2, (1,))
+    partial(chip(-1))
+    zg_pass(3, (0,))
+    steps[4]()
+    for m in range(2):
+        send_kind(m)
+    loop(0, 2, lambda k: partial(chip(4 * k - 2)))
+    steps[5]()
+    zg_pass(3, (1,))
+    loop(0, 2, lambda k: partial(chip(6 * k - 3)))
+    zg_wait(4, 0)
+    zg_wait(4, 1)
+    partial(chip(4))
+
+    def in_order(body, part=slice(None)):
+        for dx, dy in WO_ORDER[part]:
+            ox, oy = dx + core * (dy - dx), dy + core * (dx - dy)
+            body(lax.rem(x + ox, SIDE) * SIDE + lax.rem(y + oy, SIDE))
+
+    def wo_src(p):
+        return r.wo.at[pl.ds(core * 128, 128), pl.ds(pl.multiple_of(p * SH, SH), SH)]
+
+    def wo_copy(row, to):
+        return remote(wo_src(to), r.wof.at[row, core], r.wo_s.at[to], r.wo_r.at[row], tp=to)
+
+    load("wo", wo_src(t), r.wof.at[t, core])
+
+    def send_wo(n):
+        in_order(lambda p: wo_copy(t, p).start(), slice(3 * n, 3 * n + 3))
+
+    def pr_copy(block, slot, to):
+        return remote(r.ps.at[block], r.pr.at[slot], r.pr_s.at[to], r.pr_r.at[slot], tp=to)
+
+    in_order(lambda p: pr_copy(p, t, p).start())
+    r.pr[t] = r.ps[t]
+    send_wo(0)
     for ref in (r.qcat, r.vcat, r.oucat, r.qacc, r.kvacc, r.rs2s):
         ref[...] = jnp.zeros_like(ref)
-
-    def wo_src(p):
-        return r.wo.at[pl.ds(core * 128, 128), pl.ds(pl.multiple_of(p * SH, SH), SH)]
-
-    def wo_copy(row, to):
-        return remote(wo_src(to), r.wof.at[row, core], r.wo_s.at[to], r.wo_r.at[row], tp=to)
-
-    load("wo", wo_src(t), r.wof.at[t, core])
-    for n, step in enumerate(steps[2:]):
-        step()
-        for dx, dy in WO_ORDER[3 * n : 3 * n + 3]:
-            ox, oy = dx + core * (dy - dx), dy + core * (dx - dy)
-            p = lax.rem(x + ox, SIDE) * SIDE + lax.rem(y + oy, SIDE)
-            wo_copy(t, p).start()
-
-    peers(t, NT, lambda p: ss_copy(p, p).wait_recv())
-    total = jnp.sum(r.ssb[...], axis=0)
-    scale = [
-        lax.rsqrt(to_column(total[s : s + 1, :]) * (1.0 / D) + NORM_EPS) for s in range(2)
-    ]
-    for b in range(NT):
-        r.gains[b] = jnp.concatenate([r.ssb[b, 2 + q : 3 + q, :] for q in range(4)], axis=1)
-
-    def normalise(b, dst):
-        gain = r.gains[b]
-        n0, n1 = (r.ag[b, s].astype(F32) * scale[s] * gain for s in range(2))
-        for p in range(NT):
-            rows = slice(8 * p, 8 * p + 8)
-            dst[p * OWN : (p + 1) * OWN] = jnp.concatenate([n0[rows], n1[rows]], axis=0).astype(BF16)
-
-    normalise(t, r.mine)
+    steps[6]()
+
+    own_scales = scales(total)
     for name in ("wq", "wk", "wv"):
         loads[name].wait()
 
     def project(b):
         cols = pl.ds(pl.multiple_of(b * SH, SH), SH)
-        normalise(b, r.nrm)
+        normalise(r.ag.at[b], own_scales, r.gains[b])
         block = r.nrm[...]
         r.qacc[...] += dot(block, r.wqv[cols, :])
         r.kvacc[...] += dot_nt(block, r.wkv[:, cols])
 
-    loop(0, NT, project)
-
-    loads["wo"].wait()
-    peers(t, NT, lambda p: wo_copy(p, p).wait_recv())
-    sib = remote(
-        r.wof.at[:, core], r.wof.at[:, core], r.sib_s.at[0], r.sib_r.at[0], inst=sibling
-    )
-    sib.start()
-
-    def z_wait(m):
-        peers(i, NI, lambda p: z_copy(m, p, p, p).wait_recv())
-
-    def reduce_rows(own, send, recv, gathered, s1, r1, s2, r2):
-        def c1(block, slot, to):
-            return remote(send.at[block], recv.at[slot], s1.at[to], r1.at[slot], tp=to)
-
-        def c2(slot, to):
-            return remote(gathered.at[slot], gathered.at[slot], s2.at[to], r2.at[slot], tp=to)
-
-        peers(t, NT, lambda p: c1(p, t, p).start())
-        recv[t] = send[t]
-        peers(t, NT, lambda p: c1(p, p, p).wait_recv())
-        gathered[t] = jnp.sum(recv[...], axis=0).astype(BF16)
-        peers(t, NT, lambda p: c2(t, p).start())
-        peers(t, NT, lambda p: c2(p, p).wait_recv())
-
-        def finish():
-            peers(t, NT, lambda p: c1(p, p, p).wait_send())
-            peers(t, NT, lambda p: c2(p, p).wait_send())
-
-        return gathered[...].reshape(R2, 128).astype(F32), finish
-
+    loop(0, 6, project)
+    peers(t, NT, lambda p: pr_copy(p, p, p).wait_recv())
+    sums = jnp.zeros((NZ, OWN, 128), F32)
+    for b in range(NT):
+        sums += r.pr[b].astype(F32)
+    r.rrs[...] = sums.astype(BF16)
+
+    def rr_copy(block, slot, to):
+        return remote(
+            r.rrs.at[block], r.rr.at[slot], r.rr_s.at[to], r.rr_r.at[slot], inst=to * 2 + core
+        )
+
+    peers(zc, NZ, lambda p: rr_copy(p, zc, p).start())
+    r.rr[zc] = r.rrs[zc]
+    send_wo(1)
+    send_kind(2)
+    loop(6, 11, project)
+    peers(zc, NZ, lambda p: rr_copy(p, p, p).wait_recv())
+    r.rk1[t] = jnp.sum(r.rr[...].astype(F32), axis=0).astype(BF16)
+
+    def rk_copy(slot, to):
+        return remote(r.rk1.at[slot], r.rk1.at[slot], r.rk1_s.at[to], r.rk1_r.at[slot], tp=to)
+
+    peers(t, NT, lambda p: rk_copy(t, p).start())
+    send_wo(2)
+    send_kind(3)
+    loop(11, NT, project)
+    z_wait(0)
+    z_wait(1)
+    for k in range(SLOTS):
+        r.qcat[k * 128 : k * 128 + 64] = r.qur[entry(NI + k, NI)]
+        r.vcat[pl.ds(lane0, 32), k * 128 : (k + 1) * 128] = r.vur[entry(NI + k, NI)]
+    peers(t, NT, lambda p: rk_copy(p, p).wait_recv())
+    rank = r.rk1[...].reshape(R2, 128).astype(F32)
     slot_of_row = r.rmask[...]
-    z_wait(0)
-    mine = r.mine[...]
-    part = jnp.zeros((R2, 128), F32)
-    for k in range(SLOTS):
-        got = dot(mine, r.dnr[entry(NI + k, NI)])
-        part = jnp.where(slot_of_row == float(k), got, part)
-    r.rs1s[...] = part.reshape(NT, OWN, 128)
-    rank, finish1 = reduce_rows(
-        t, r.rs1s, r.rs1r, r.rk1, r.rs1_s, r.rs1_r, r.rk1_s, r.rk1_r
-    )
     rolled = pltpu.roll(rank, 64, 1)
     for k in range(SLOTS):
         cols = slice(k * 128, (k + 1) * 128)
         r.rall[:, cols] = jnp.where(slot_of_row == float(k), rank, 0.0).astype(BF16)
         r.rall2[:, cols] = jnp.where(slot_of_row == float(k), rolled, 0.0).astype(BF16)
 
-    z_wait(1)
-    z_wait(2)
-    for k in range(SLOTS):
-        r.qcat[k * 128 : k * 128 + 64] = r.qur[entry(NI + k, NI)]
-        r.vcat[pl.ds(lane0, 32), k * 128 : (k + 1) * 128] = r.vur[entry(NI + k, NI)]
     query = r.qacc[...] + ADAPTER_SCALING * dot(r.rall[...], r.qcat[...])
     fresh_value = r.kvacc[:, 128:] + ADAPTER_SCALING * dot_nt(r.rall2[...], r.vcat[...])
     r.qkvs[:, :, 0:256] = query.astype(BF16).reshape(NT, OWN, 256)
@@ -442,6 +551,8 @@
 
     peers(t, NT, lambda p: qkv_copy(p, t, p).start())
     r.qkvr[t] = r.qkvs[t]
+    send_wo(3)
+    send_wo(4)
 
     row = lax.broadcasted_iota(jnp.int32, (OWN, HD), 0)
     lane = lax.broadcasted_iota(jnp.int32, (OWN, HD), 1)
@@ -516,9 +627,8 @@
     start, steps, sent2 = mesh_gather(x, y, ag2_ref, r.ag2_s, r.ag2_r)
     start()
     r.attd[t] = r.ag2[t, :, pl.ds(pl.multiple_of(t * 256, 256), 256)]
-    z_wait(3)
     steps[0]()
-    steps[1]()
+    z_wait(2)
     peers(t, NT, lambda p: at_copy(p, p, p).wait_recv())
     heads = r.attd[...].reshape(R2, 256)
     part = jnp.zeros((R2, 64), F32)
@@ -526,15 +636,27 @@
         got = dot_nt(heads, r.odr[entry(NI + k, NI)])
         part = jnp.where(slot_of_row[:, :64] == float(k), got, part)
     r.rs2s[:, :, 0:64] = part.reshape(NT, OWN, 64)
-    for step in steps[2:4]:
-        step()
-    rank, finish2 = reduce_rows(
-        t, r.rs2s, r.rs2r, r.rk2, r.rs2_s, r.rs2_r, r.rk2_s, r.rk2_r
+
+    def c1(block, slot, to):
+        return remote(r.rs2s.at[block], r.rs2r.at[slot], r.rs2_s.at[to], r.rs2_r.at[slot], tp=to)
+
+    def c2(slot, to):
+        return remote(r.rk2.at[slot], r.rk2.at[slot], r.rk2_s.at[to], r.rk2_r.at[slot], tp=to)
+
+    peers(t, NT, lambda p: c1(p, t, p).start())
+    r.rs2r[t] = r.rs2s[t]
+    steps[1]()
+    steps[2]()
+    loads["wo"].wait()
+    peers(t, NT, lambda p: wo_copy(p, p).wait_recv())
+    sib = remote(
+        r.wof.at[:, core], r.wof.at[:, core], r.sib_s.at[0], r.sib_r.at[0], inst=sibling
     )
-    for k in range(SLOTS):
-        cols = slice(k * 128, (k + 1) * 128)
-        r.rall[:, cols] = jnp.where(slot_of_row == float(k), rank, 0.0).astype(BF16)
-    for step in steps[4:]:
+    sib.start()
+    peers(t, NT, lambda p: c1(p, p, p).wait_recv())
+    r.rk2[t] = jnp.sum(r.rs2r[...], axis=0).astype(BF16)
+    peers(t, NT, lambda p: c2(t, p).start())
+    for step in steps[3:]:
         step()
 
     sib_in = remote(
@@ -549,7 +671,12 @@
         r.oacc[...] += dot(lhs, rhs)
 
     loop(0, 8, out_chunk)
-    z_wait(4)
+    peers(t, NT, lambda p: c2(p, p).wait_recv())
+    rank = r.rk2[...].reshape(R2, 128).astype(F32)
+    for k in range(SLOTS):
+        cols = slice(k * 128, (k + 1) * 128)
+        r.rall[:, cols] = jnp.where(slot_of_row == float(k), rank, 0.0).astype(BF16)
+    z_wait(3)
     for k in range(SLOTS):
         r.oucat[k * 128 : k * 128 + 64] = r.our[entry(NI + k, NI)]
     res = r.oacc[...] + ADAPTER_SCALING * dot(r.rall[...], r.oucat[...])
@@ -561,16 +688,20 @@
         r.out[s] = r.oacc[s * ROWS : (s + 1) * ROWS].astype(BF16)
 
     peers(t, NT, lambda p: ss_copy(p, p).wait_send())
-    for m in range(5):
+    for m in range(4):
         peers(i, NI, lambda p, m=m: z_copy(m, p, p, p).wait_send())
-    for c in sent1 + sent2:
+    for c in sent1 + sent2 + sent_z + [dn_out]:
         c.wait_send()
+    peers(zc, NZ, lambda p: zs_copy(p, p).wait_send())
+    peers(t, NT, lambda p: pr_copy(p, p, p).wait_send())
+    peers(zc, NZ, lambda p: rr_copy(p, p, p).wait_send())
+    peers(t, NT, lambda p: rk_copy(p, p).wait_send())
     peers(t, NT, lambda p: wo_copy(p, p).wait_send())
     sib.wait_send()
     peers(t, NT, lambda p: qkv_copy(p, p, p).wait_send())
     peers(t, NT, lambda p: at_copy(p, p, p).wait_send())
-    finish1()
-    finish2()
+    peers(t, NT, lambda p: c1(p, p, p).wait_send())
+    peers(t, NT, lambda p: c2(p, p).wait_send())
 
 
 def local(

time: 123 us -> 113 us (0.919)
  Pallas kernels: 121 us -> 110 us
    pallas_call x1, Pallas kernels: 121 us -> 110 us  [local(): pl.pallas_call(kernel, out_shape=jax.ShapeDtypeStruct((2, ROWS, SH), BF16...]
where the time goes in v3:
time: 113 us; the launch traced here: 112 us
  Pallas kernels  110 us (97%)
  local copies, waits for them, and re-layouts  1.67 us (1%)
    pallas_call x1, Pallas kernels, local(): pl.pallas_call(kernel, out_shape=jax.ShapeDtypeStruct((2, ROWS, SH), BF16...  110 us

profile of v3, /device:TPU:2, one launch (start us, length us, event | category | flops | bytes accessed | tf_op | source)
XLA Modules:
  0.0 112.1 jit_solution(6386007716528765347)
XLA Ops:
  0.0 110.5 %decode_block.1 = bf16[2,128,512]{2,1,0:T(8,128)(2,1)} custom-call(s32[8]{0:T(128)} %args_0_.4, bf16[4,128]{1,0:T(4,128)(2,1)} %bitcast.10, s32[1,128]{1,0:T(1,128)} %bitcast.11, s32[1,128]{1,0:T(1,128)} %bitcast.12, s32[1,128]{1,0:T(1,128)} %bitcast.13, bf16[2,128,512]{2,1,0:T(8,128)(2,1)} %args_5_.4, bf16[8192,256]{1,0:T(8,128)(2,1)} %args_6_.4, ...), custom_call_target="tpu_custom_call" | custom-call | tf_op jit(solution)/shard_map/decode_block/pallas_call | solution.py:729
  110.5 1.7 %copy.19 = bf16[2,128,512]{2,1,0:T(8,128)(2,1)} copy(bf16[2,128,512]{2,1,0:T(8,128)(2,1)} %decode_block.1) | data formatting | bytes 524288

commit v4 on v3

--- a/solution.py
+++ b/solution.py
@@ -450,40 +450,42 @@
     partial(chip(1))
     zg_pass(2, (1,))
     partial(chip(-1))
+    def in_order(body, part=slice(None)):
+        for dx, dy in WO_ORDER[part]:
+            ox, oy = dx + core * (dy - dx), dy + core * (dx - dy)
+            body(lax.rem(x + ox, SIDE) * SIDE + lax.rem(y + oy, SIDE))
+
+    def wo_src(p):
+        return r.wo.at[pl.ds(core * 128, 128), pl.ds(pl.multiple_of(p * SH, SH), SH)]
+
+    def wo_copy(row, to):
+        return remote(wo_src(to), r.wof.at[row, core], r.wo_s.at[to], r.wo_r.at[row], tp=to)
+
+    load("wo", wo_src(t), r.wof.at[t, core])
+
+    def send_wo(n):
+        in_order(lambda p: wo_copy(t, p).start(), slice(3 * n, 3 * n + 3))
+
     zg_pass(3, (0,))
     steps[4]()
+    send_wo(0)
     for m in range(2):
         send_kind(m)
     loop(0, 2, lambda k: partial(chip(4 * k - 2)))
     steps[5]()
+    send_wo(1)
     zg_pass(3, (1,))
     loop(0, 2, lambda k: partial(chip(6 * k - 3)))
     zg_wait(4, 0)
     zg_wait(4, 1)
     partial(chip(4))
 
-    def in_order(body, part=slice(None)):
-        for dx, dy in WO_ORDER[part]:
-            ox, oy = dx + core * (dy - dx), dy + core * (dx - dy)
-            body(lax.rem(x + ox, SIDE) * SIDE + lax.rem(y + oy, SIDE))
-
-    def wo_src(p):
-        return r.wo.at[pl.ds(core * 128, 128), pl.ds(pl.multiple_of(p * SH, SH), SH)]
-
-    def wo_copy(row, to):
-        return remote(wo_src(to), r.wof.at[row, core], r.wo_s.at[to], r.wo_r.at[row], tp=to)
-
-    load("wo", wo_src(t), r.wof.at[t, core])
-
-    def send_wo(n):
-        in_order(lambda p: wo_copy(t, p).start(), slice(3 * n, 3 * n + 3))
-
     def pr_copy(block, slot, to):
         return remote(r.ps.at[block], r.pr.at[slot], r.pr_s.at[to], r.pr_r.at[slot], tp=to)
 
     in_order(lambda p: pr_copy(p, t, p).start())
     r.pr[t] = r.ps[t]
-    send_wo(0)
+    send_wo(2)
     for ref in (r.qcat, r.vcat, r.oucat, r.qacc, r.kvacc, r.rs2s):
         ref[...] = jnp.zeros_like(ref)
     steps[6]()
@@ -513,7 +515,7 @@
 
     peers(zc, NZ, lambda p: rr_copy(p, zc, p).start())
     r.rr[zc] = r.rrs[zc]
-    send_wo(1)
+    send_wo(3)
     send_kind(2)
     loop(6, 11, project)
     peers(zc, NZ, lambda p: rr_copy(p, p, p).wait_recv())
@@ -523,7 +525,7 @@
         return remote(r.rk1.at[slot], r.rk1.at[slot], r.rk1_s.at[to], r.rk1_r.at[slot], tp=to)
 
     peers(t, NT, lambda p: rk_copy(t, p).start())
-    send_wo(2)
+    send_wo(4)
     send_kind(3)
     loop(11, NT, project)
     z_wait(0)
@@ -551,8 +553,6 @@
 
     peers(t, NT, lambda p: qkv_copy(p, t, p).start())
     r.qkvr[t] = r.qkvs[t]
-    send_wo(3)
-    send_wo(4)
 
     row = lax.broadcasted_iota(jnp.int32, (OWN, HD), 0)
     lane = lax.broadcasted_iota(jnp.int32, (OWN, HD), 1)
@@ -569,6 +569,13 @@
     def rotate(v):
         return v * cos2 + pltpu.roll(v, 64, 1) * sin2
 
+    peers(t, NT, lambda p: ss_copy(p, p).wait_send())
+    for c in sent1 + sent_z + [dn_out]:
+        c.wait_send()
+    peers(zc, NZ, lambda p: zs_copy(p, p).wait_send())
+    peers(t, NT, lambda p: pr_copy(p, p, p).wait_send())
+    peers(zc, NZ, lambda p: rr_copy(p, p, p).wait_send())
+    peers(t, NT, lambda p: rk_copy(p, p).wait_send())
     peers(t, NT, lambda p: qkv_copy(p, p, p).wait_recv())
     loads["kc"].wait()
     loads["vc"].wait()
@@ -656,6 +663,10 @@
     peers(t, NT, lambda p: c1(p, p, p).wait_recv())
     r.rk2[t] = jnp.sum(r.rs2r[...], axis=0).astype(BF16)
     peers(t, NT, lambda p: c2(t, p).start())
+    peers(t, NT, lambda p: qkv_copy(p, p, p).wait_send())
+    peers(t, NT, lambda p: wo_copy(p, p).wait_send())
+    for m in range(3):
+        peers(i, NI, lambda p, m=m: z_copy(m, p, p, p).wait_send())
     for step in steps[3:]:
         step()
 
@@ -687,18 +698,10 @@
     for s in range(2):
         r.out[s] = r.oacc[s * ROWS : (s + 1) * ROWS].astype(BF16)
 
-    peers(t, NT, lambda p: ss_copy(p, p).wait_send())
-    for m in range(4):
-        peers(i, NI, lambda p, m=m: z_copy(m, p, p, p).wait_send())
-    for c in sent1 + sent2 + sent_z + [dn_out]:
+    for c in sent2:
         c.wait_send()
-    peers(zc, NZ, lambda p: zs_copy(p, p).wait_send())
-    peers(t, NT, lambda p: pr_copy(p, p, p).wait_send())
-    peers(zc, NZ, lambda p: rr_copy(p, p, p).wait_send())
-    peers(t, NT, lambda p: rk_copy(p, p).wait_send())
-    peers(t, NT, lambda p: wo_copy(p, p).wait_send())
+    peers(i, NI, lambda p: z_copy(3, p, p, p).wait_send())
     sib.wait_send()
-    peers(t, NT, lambda p: qkv_copy(p, p, p).wait_send())
     peers(t, NT, lambda p: at_copy(p, p, p).wait_send())
     peers(t, NT, lambda p: c1(p, p, p).wait_send())
     peers(t, NT, lambda p: c2(p, p).wait_send())

time: 113 us -> 109 us (0.965)
  Pallas kernels: 110 us -> 107 us
    pallas_call x1, Pallas kernels: 110 us -> 107 us  [local(): pl.pallas_call(kernel, out_shape=jax.ShapeDtypeStruct((2, ROWS, SH), BF16...]
where the time goes in v4:
time: 109 us
  Pallas kernels  107 us (98%)
  local copies, waits for them, and re-layouts  1.67 us (2%)
    pallas_call x1, Pallas kernels, local(): pl.pallas_call(kernel, out_shape=jax.ShapeDtypeStruct((2, ROWS, SH), BF16...  107 us

profile of v4, /device:TPU:2, one launch (start us, length us, event | category | flops | bytes accessed | tf_op | source)
XLA Modules:
  0.0 108.5 jit_solution(10898175436144871160)
XLA Ops:
  0.0 106.8 %decode_block.1 = bf16[2,128,512]{2,1,0:T(8,128)(2,1)} custom-call(s32[8]{0:T(128)} %args_0_.4, bf16[4,128]{1,0:T(4,128)(2,1)} %bitcast.10, s32[1,128]{1,0:T(1,128)} %bitcast.11, s32[1,128]{1,0:T(1,128)} %bitcast.12, s32[1,128]{1,0:T(1,128)} %bitcast.13, bf16[2,128,512]{2,1,0:T(8,128)(2,1)} %args_5_.4, bf16[8192,256]{1,0:T(8,128)(2,1)} %args_6_.4, ...), custom_call_target="tpu_custom_call" | custom-call | tf_op jit(solution)/shard_map/decode_block/pallas_call | solution.py:732
  106.8 1.7 %copy.19 = bf16[2,128,512]{2,1,0:T(8,128)(2,1)} copy(bf16[2,128,512]{2,1,0:T(8,128)(2,1)} %decode_block.1) | data formatting | bytes 524288

commit v5 on v4

--- a/solution.py
+++ b/solution.py
@@ -516,7 +516,6 @@
     peers(zc, NZ, lambda p: rr_copy(p, zc, p).start())
     r.rr[zc] = r.rrs[zc]
     send_wo(3)
-    send_kind(2)
     loop(6, 11, project)
     peers(zc, NZ, lambda p: rr_copy(p, p, p).wait_recv())
     r.rk1[t] = jnp.sum(r.rr[...].astype(F32), axis=0).astype(BF16)
@@ -526,6 +525,7 @@
 
     peers(t, NT, lambda p: rk_copy(t, p).start())
     send_wo(4)
+    send_kind(2)
     send_kind(3)
     loop(11, NT, project)
     z_wait(0)

time: 109 us -> 109 us (level)
  no operation moved by 1% of the time
where the time goes in v5:
time: 109 us; the launch traced here: 108 us
  Pallas kernels  107 us (98%)
  local copies, waits for them, and re-layouts  1.67 us (2%)
    pallas_call x1, Pallas kernels, local(): pl.pallas_call(kernel, out_shape=jax.ShapeDtypeStruct((2, ROWS, SH), BF16...  107 us

profile of v5, /device:TPU:2, one launch (start us, length us, event | category | flops | bytes accessed | tf_op | source)
XLA Modules:
  0.0 108.3 jit_solution(6888038479781206685)
XLA Ops:
  0.0 106.7 %decode_block.1 = bf16[2,128,512]{2,1,0:T(8,128)(2,1)} custom-call(s32[8]{0:T(128)} %args_0_.4, bf16[4,128]{1,0:T(4,128)(2,1)} %bitcast.10, s32[1,128]{1,0:T(1,128)} %bitcast.11, s32[1,128]{1,0:T(1,128)} %bitcast.12, s32[1,128]{1,0:T(1,128)} %bitcast.13, bf16[2,128,512]{2,1,0:T(8,128)(2,1)} %args_5_.4, bf16[8192,256]{1,0:T(8,128)(2,1)} %args_6_.4, ...), custom_call_target="tpu_custom_call" | custom-call | tf_op jit(solution)/shard_map/decode_block/pallas_call | solution.py:732
  106.7 1.7 %copy.19 = bf16[2,128,512]{2,1,0:T(8,128)(2,1)} copy(bf16[2,128,512]{2,1,0:T(8,128)(2,1)} %decode_block.1) | data formatting | bytes 524288
